TPU v7x, 256 devices: a whole 4x4x8 slice. The times are simulated.
256 devices in a mesh: query: 8 (over x_hi, y), passage: 32 (over z, x_lo, core).
Axes of the slice: x: 4 (x_hi: 2, x_lo: 2; x = x_hi * 2 + x_lo), y: 4, z: 8, core: 2. Of those that a mesh axis runs over, the one named last changes fastest.
Arguments:
- queries: bfloat16 [32768, 4096], P(('query', 'passage')), may hold values from -32 to 32
- passages: bfloat16 [1024, 4096], P('passage'), may hold values from -8 to 8
- candidates: int32 [32768, 128], P(('query', 'passage')), may hold values from 0 to 1023, as said below
- teacher_scores: float32 [32768, 128], P(('query', 'passage')), may hold values from -20 to 260
Outputs:
- query_loss: float32 [32768], P(('query', 'passage'))
- grad_queries: float32 [32768, 4096], P(('query', 'passage'))
- grad_passages: float32 [1024, 4096], P('passage', 'query')
Inputs may be any that keep to these rules, and one draw needn't show every extreme that they name: Each row holds 128 different indices in rising order, so that a query's candidates come grouped by the passage shard that holds them; some shards of the pool are named far more often than others.
All inputs are finite; a program needn't handle non-finite values.
Results may differ from a plain program's by a relative error of at most 0.0028.
Values may be sent and summed in bfloat16 or wider, within the bound.
A program may use at most 128 MiB of HBM per device.

v0:
```python
import math

import jax
import jax.numpy as jnp
from jax import lax
from jax.sharding import PartitionSpec as P

W1 = 64
W2 = 256
W3 = 1024


def segment_bounds(full_width):
    return (0, W1, W2, W3, full_width)


def split_columns(rows):
    bounds = segment_bounds(rows.shape[1])
    return [rows[:, bounds[segment] : bounds[segment + 1]] for segment in range(4)]


def piece_logits(query_parts, shard_rows, first_row, chosen):
    shard_parts = split_columns(shard_rows)
    offset = chosen - first_row
    inside = (offset >= 0) & (offset < shard_rows.shape[0])
    clipped = jnp.clip(offset, 0, shard_rows.shape[0] - 1)
    running = None
    picked = []
    for segment in range(4):
        product = jnp.einsum(
            "qd,pd->qp",
            query_parts[segment],
            shard_parts[segment],
            preferred_element_type=jnp.float32,
        )
        running = product if running is None else running + product
        picked.append(jnp.take_along_axis(running, clipped, axis=1))
    stacked = jnp.stack(picked)
    return jnp.where(inside[None], stacked, jnp.zeros_like(stacked))


def head_terms(logits, scores, full_width):
    widths = (W1, W2, W3, full_width)
    scales = jnp.array([1.0 / math.sqrt(value) for value in widths], jnp.float32)[:, None, None]
    log_teacher = jax.nn.log_softmax(scores, axis=-1)
    teacher = jnp.exp(log_teacher)
    student = jax.nn.log_softmax(logits * scales, axis=-1)
    query_loss = jnp.sum(teacher[None] * (log_teacher[None] - student), axis=(0, 2))
    dlogit = (jnp.exp(student) - teacher[None]) * scales
    tail_two = dlogit[2] + dlogit[3]
    tail_one = dlogit[1] + tail_two
    coefficient = jnp.stack([dlogit[0] + tail_one, tail_one, tail_two, dlogit[3]]).astype(
        jnp.bfloat16
    )
    return (query_loss, coefficient)


def spread_flipped(coefficient, chosen, pool_size):
    row_ids = jnp.broadcast_to(jnp.arange(chosen.shape[0], dtype=jnp.int32)[:, None], chosen.shape)
    empty = jnp.zeros((4, pool_size, chosen.shape[0]), jnp.bfloat16)
    return empty.at[:, chosen, row_ids].set(coefficient)


def query_gradient(flipped, shard_rows):
    shard_parts = split_columns(shard_rows)
    products = []
    for segment in range(4):
        window = flipped[segment]
        products.append(
            jnp.einsum(
                "pq,pd->qd", window, shard_parts[segment], preferred_element_type=jnp.float32
            )
        )
    return jnp.concatenate(products, axis=1)


def passage_term(flipped, query_parts):
    products = []
    for segment in range(4):
        window = flipped[segment]
        products.append(jnp.dot(window, query_parts[segment], preferred_element_type=jnp.float32))
    return jnp.concatenate(products, axis=1)


def shards(queries, passages, candidates, teacher_scores):
    full_width = queries.shape[1]
    shard_size = passages.shape[0]
    pool_size = shard_size * lax.axis_size("passage")
    query_parts = split_columns(queries)
    passage_pool = lax.all_gather(passages, "passage", axis=0, tiled=True)
    logits = piece_logits(query_parts, passage_pool, 0, candidates)
    query_loss, coefficient = head_terms(logits, teacher_scores, full_width)
    flipped = spread_flipped(coefficient, candidates, pool_size)
    grad_queries = query_gradient(flipped, passage_pool)
    row_sums = lax.psum_scatter(
        passage_term(flipped, query_parts), "passage", scatter_dimension=0, tiled=True
    )
    grad_passages = lax.psum_scatter(row_sums, "query", scatter_dimension=1, tiled=True)
    return (query_loss, grad_queries, grad_passages)


def solution(mesh):
    return jax.shard_map(
        shards,
        mesh=mesh,
        in_specs=(
            P(("query", "passage"), None),
            P("passage", None),
            P(("query", "passage"), None),
            P(("query", "passage"), None),
        ),
        out_specs=(P(("query", "passage")), P(("query", "passage"), None), P("passage", "query")),
        check_vma=False,
    )
```

profile of v0, /device:TPU:1, one launch (start us, length us, event | category | flops | bytes accessed | tf_op | source)
XLA Modules:
  0.0 1171.4 jit_solution(16152431084080095663)
XLA Ops:
  7.9 0.9 reduce_max.20
  8.9 1.0 exponential_reduce_fusion.1
  9.9 0.9 fusion.50
  11.5 0.8 and_reduce_fusion
  12.3 7.1 sort
  19.5 0.9 compare_and_fusion.1
  20.4 0.9 fusion.67
  21.3 0.9 fusion.56
  22.2 64.2 %all-gather.2.cloned.1.call-done = bf16[1024,4096]{1,0:T(8,128)(2,1)} async-done(((bf16[32,4096]{1,0:T(8,128)(2,1)}), bf16[1024,4096]{1,0:T(8,128)(2,1)}) %all-gather.2.cloned.1.call-update) | async-done | bytes 8388624 | tf_op jit(solution)/shard_map/all_gather | solution.py:90
  86.4 1.2 fusion.46
  87.6 129.9 %gather_fusion = f32[16384]{0:T(1024)S(1)} fusion(f32[128,1024]{1,0:T(8,128)S(1)} %fusion.46, s32[16384]{0:T(1024)S(1)} %fusion.56), kind=kCustom, calls=%fused_computation.clone | custom fusion | bytes 262144 | tf_op jit(solution)/shard_map/jit(take_along_axis)/gather | solution.py:37
  217.6 1.5 convolution_add_fusion
  219.2 129.5 %gather_fusion.1 = f32[16384]{0:T(1024)S(1)} fusion(f32[128,1024]{1,0:T(8,128)S(1)} %convolution_add_fusion, s32[16384]{0:T(1024)S(1)} %fusion.56), kind=kCustom, calls=%fused_computation.1.clone | custom fusion | bytes 262144 | tf_op jit(solution)/shard_map/jit(take_along_axis)/gather | solution.py:37
  348.6 2.0 fusion.16
  350.7 129.5 %gather_fusion.2 = f32[16384]{0:T(1024)S(1)} fusion(f32[128,1024]{1,0:T(8,128)S(1)} %fusion.16, s32[16384]{0:T(1024)S(1)} %fusion.56), kind=kCustom, calls=%fused_computation.2.clone | custom fusion | bytes 262144 | tf_op jit(solution)/shard_map/jit(take_along_axis)/gather | solution.py:37
  480.2 5.0 fusion.19
  485.2 129.5 %gather_fusion.3 = f32[16384]{0:T(1024)S(1)} fusion(f32[128,1024]{1,0:T(8,128)S(1)} %fusion.19, s32[16384]{0:T(1024)S(1)} %fusion.56), kind=kCustom, calls=%fused_computation.3.clone | custom fusion | bytes 262144 | tf_op jit(solution)/shard_map/jit(take_along_axis)/gather | solution.py:37
  614.9 0.8 subtract_multiply_fusion
  615.8 3.3 copy.25
  619.1 167.9 %scatter_custom_fusion = bf16[4,131072]{0,1:T(8,128)(2,1)} fusion(s32[16384]{0:T(1024)S(1)} %get-tuple-element.4, bf16[]{:T(256)} %constant.23.clone.1, bf16[16384,4]{1,0:T(8,128)(2,1)} %bitcast.64, s32[16384]{0:T(1024)S(1)} %broadcast_clamp_fusion), kind=kCustom, calls=%fused_computation.12 | custom fusion | bytes 1049088
  787.0 81.9 %slice_reduce_fusion = (bf16[131072]{0:T(1024)(128)(2,1)S(1)}, bf16[131072]{0:T(1024)(128)(2,1)S(1)}, bf16[131072]{0:T(1024)(128)(2,1)S(1)}, bf16[131072]{0:T(1024)(128)(2,1)S(1)}) fusion(bf16[4,131072]{0,1:T(8,128)(2,1)} %scatter_custom_fusion), kind=kLoop, calls=%fused_computation.8 | loop fusion | bytes 2097152 | tf_op jit(solution)/shard_map/slice | solution.py:68
  868.9 1.1 fusion.40
  870.0 1.3 fusion.37
  871.9 6.3 fusion.25
  878.3 18.2 %concatenate.11 = f32[1024,4096]{1,0:T(8,128)} concatenate(f32[1024,64]{1,0:T(8,128)} %fusion.40, f32[1024,192]{1,0:T(8,128)} %fusion.37, f32[1024,768]{1,0:T(8,128)S(1)} %fusion.34, f32[1024,3072]{1,0:T(8,128)} %fusion.25), dimensions={1} | concatenate | bytes 33554432 | tf_op jit(solution)/shard_map/concatenate | solution.py:82
  896.5 188.8 %reduce-scatter.3.cloned.1.call-done = f32[32,4096]{1,0:T(8,128)} async-done(((f32[1024,4096]{1,0:T(8,128)}), f32[32,4096]{1,0:T(8,128)}) %reduce-scatter.3.cloned.1.call-update) | async-done | bytes 524304 | tf_op jit(solution)/shard_map/reduce_scatter | solution.py:95
  1085.4 1.2 fusion.42
  1086.6 1.6 fusion.28
  1088.2 1.8 fusion.12
  1090.0 3.8 fusion.5
  1093.8 2.1 concatenate.10
  1095.9 68.5 %reduce-scatter.5.cloned.1.call-done = f32[32,512]{1,0:T(8,128)} async-done(((f32[32,4096]{1,0:T(8,128)}), f32[32,512]{1,0:T(8,128)}) %reduce-scatter.5.cloned.1.call-update) | async-done | bytes 65552 | tf_op jit(solution)/shard_map/reduce_scatter | solution.py:98
  (39 shorter events, 2.5 us)
Async XLA Ops:
  7.2 79.2 %all-gather.2.cloned.1.call-start = ((), (), s32[]{:S(2)}) async-start(), calls=%async_computation.2 | async-start | bytes 8650752 | tf_op jit(solution)/shard_map/all_gather | solution.py:90
  7.9 1077.4 %reduce-scatter.3.cloned.1.call-start = ((), (), s32[]{:S(2)}) async-start(), calls=%async_computation.3 | async-start | bytes 17301504 | tf_op jit(solution)/shard_map/reduce_scatter | solution.py:95
  87.6 130.0 %copy-start.8 = (s32[128,128]{1,0:T(8,128)S(1)}, s32[128,128]{1,0:T(8,128)}, u32[]{:S(2)}) copy-start(s32[128,128]{1,0:T(8,128)} %param.9) | copy-start | bytes 196612
  87.6 130.0 %copy-start.6 = (bf16[128,4096]{1,0:T(8,128)(2,1)S(1)}, bf16[128,4096]{1,0:T(8,128)(2,1)}, u32[]{:S(2)}) copy-start(bf16[128,4096]{1,0:T(8,128)(2,1)} %param.7) | copy-start | bytes 3145732
  485.2 129.5 %copy-start.9 = (f32[4]{0:T(128)S(1)}, f32[4]{0:T(128)}, u32[]{:S(2)}) copy-start(f32[4]{0:T(128)} %constant.27.clone) | copy-start | bytes 52
  787.0 84.4 %copy-start.7 = (bf16[128,4096]{1,0:T(8,128)(2,1)S(1)}, bf16[128,4096]{1,0:T(8,128)(2,1)}, u32[]{:S(2)}) copy-start(bf16[128,4096]{1,0:T(8,128)(2,1)} %param.7) | copy-start | bytes 3145732
  868.9 2.5 copy-start
  868.9 3.0 copy-start.2
  868.9 3.0 copy-start.4
  896.4 188.9 %copy-start.3 = (bf16[131072]{0:T(1024)(128)(2,1)S(1)}, bf16[131072]{0:T(1024)(128)(2,1)}, u32[]{:S(2)}) copy-start(bf16[131072]{0:T(1024)(128)(2,1)} %copy-done.2) | copy-start | bytes 786436
  896.5 190.1 %copy-start.5 = (bf16[131072]{0:T(1024)(128)(2,1)S(1)}, bf16[131072]{0:T(1024)(128)(2,1)}, u32[]{:S(2)}) copy-start(bf16[131072]{0:T(1024)(128)(2,1)} %copy-done.4) | copy-start | bytes 786436
  896.5 191.7 %copy-start.1 = (bf16[131072]{0:T(1024)(128)(2,1)S(1)}, bf16[131072]{0:T(1024)(128)(2,1)}, u32[]{:S(2)}) copy-start(bf16[131072]{0:T(1024)(128)(2,1)} %copy-done) | copy-start | bytes 786436
  896.5 267.9 %reduce-scatter.5.cloned.1.call-start = ((), (), s32[]{:S(2)}) async-start(), calls=%async_computation.4 | async-start | bytes 589824 | tf_op jit(solution)/shard_map/reduce_scatter | solution.py:98
Sparse Core Ops, SparseCore 0:
  9.9 76.4 all-gather.1
  896.6 188.6 reduce-scatter.2
  1089.7 74.6 reduce-scatter.4
where the time goes:
time: 1180 us; the launch traced here: 1170 us
  local copies, waits for them, and re-layouts  792 us (67%)
  waiting for transfers between devices  322 us (27%)
  matrix products  27.4 us (2%)
  other arithmetic  15.3 us (1%)
  between operations  14.5 us (1%)
    gather x4, local copies, waits for them, and re-layouts, piece_logits(): picked.append(jnp.take_along_axis(running, clipped, axis=1))  518 us
    reduce_scatter x1, waiting for transfers between devices, shards(): lax.psum_scatter(passage_term(flipped, query_parts), 'passage', scatter_d...  189 us
    unnamed x22, local copies, waits for them, and re-layouts  168 us
    slice x1, local copies, waits for them, and re-layouts, query_gradient(): window = flipped[segment]  81.9 us
    reduce_scatter x1, waiting for transfers between devices, shards(): lax.psum_scatter(row_sums, 'query', scatter_dimension=1, tiled=True)  68.5 us
    all_gather x1, waiting for transfers between devices, shards(): passage_pool = lax.all_gather(passages, 'passage', axis=0, tiled=True)  64.2 us
  transfers between devices with their start and end apart: 3, of which 3 were waited for; matrix products, arithmetic and copies ran while one was open for 2% of the time, Pallas kernels for 0%

commit v1 on v0

v1 whole, which is shorter than its diff:
```python
import functools
import math

import jax
import jax.numpy as jnp
from jax import lax
from jax.experimental import pallas as pl
from jax.experimental.pallas import tpu as pltpu
from jax.sharding import PartitionSpec as P

MESH = pl.DeviceIdType.MESH
BF16 = jnp.bfloat16
F32 = jnp.float32

E = 4096
W1, W2, W3 = 64, 256, 1024
WIDTHS = (W1, W2, W3, E)
ROWS = 128
SPAN = 32
HALF = 16
NX, NY, NZ = 4, 4, 8
POOL = 2 * NZ * SPAN
GROUP = NZ * SPAN
LANES = 128
BIG = 3.0e38

QUARTER = 384
FLAT = E - 4 * QUARTER

BLOCK = 512
WA = 256
WB = BLOCK - WA


def place():
    query = lax.axis_index("query")
    passage = lax.axis_index("passage")
    x = (query // 4) * 2 + (passage // 2) % 2
    return x, query % 4, passage // 4, passage % 2


def device(x, y, z, core):
    x, y, z = x % NX, y % NY, z % NZ
    return ((x // 2) * 4 + y, (z * 2 + x % 2) * 2 + core)


def prep_kernel(candidates, scores, dense, entropy):
    x, y, z, core = place()
    raw = scores[...]
    shifted = raw - jnp.max(raw, axis=1, keepdims=True)
    log_teacher = shifted - jnp.log(jnp.sum(jnp.exp(shifted), axis=1, keepdims=True))
    teacher = jnp.exp(log_teacher)
    entropy[...] = jnp.broadcast_to(
        jnp.sum(teacher * log_teacher, axis=1, keepdims=True), (ROWS, LANES)
    )
    chosen = candidates[...]
    lane = lax.broadcasted_iota(jnp.int32, (ROWS, LANES), 1)
    for half in range(2):
        for chunk in range(POOL // LANES):
            slot = lane // SPAN + chunk * (LANES // SPAN)
            dxl, dz = slot // NZ, slot % NZ
            owner = (((z + dz) % NZ) * 2 + (x + dxl) % 2) * 2 + half
            target = owner * SPAN + lane % SPAN
            position = jnp.zeros((ROWS, LANES), jnp.int32)
            for step in (64, 32, 16, 8, 4, 2, 1):
                probe = jnp.take_along_axis(chosen, position + (step - 1), axis=1)
                position = jnp.where(probe < target, position + step, position)
            hit = jnp.take_along_axis(chosen, position, axis=1) == target
            value = jnp.take_along_axis(teacher, position, axis=1)
            dense[half, :, chunk * LANES : (chunk + 1) * LANES] = jnp.where(hit, value, -1.0)


def prepare(candidates, scores):
    return pl.pallas_call(
        prep_kernel,
        out_shape=(
            jax.ShapeDtypeStruct((2, ROWS, POOL), F32),
            jax.ShapeDtypeStruct((ROWS, LANES), F32),
        ),
        in_specs=[pl.BlockSpec(memory_space=pltpu.VMEM)] * 2,
        out_specs=(pl.BlockSpec(memory_space=pltpu.VMEM),) * 2,
        name="prepare",
    )(candidates, scores)


SCRATCH = dict(
    qs=((2 * ROWS, E), BF16),
    ws=((2 * GROUP, E), BF16),
    tt=((2 * ROWS, POOL), F32),
    lv=((4, 2 * ROWS, POOL), F32),
    st=((2 * ROWS, LANES), F32),
    sr=((2 * ROWS, LANES), F32),
    grid=((4, 2 * ROWS, POOL), BF16),
    go=((ROWS, E), F32),
    gs=((ROWS, E), F32),
    gr=((ROWS, E), F32),
    pa=((NZ, 2, 8, SPAN, WA), F32),
    pab=((NZ, 2, 8, SPAN, WA), BF16),
    ra=((2, 4, 2, 8, SPAN, WA), BF16),
    fa=((2, 2, 4, SPAN, WA), F32),
    rax=((3, 4, SPAN, WA), F32),
    ga=((4, SPAN, WA), F32),
    ray=((3, SPAN, WA), F32),
    pb=((2, 2, 4, NZ, HALF, WB), F32),
    pbb=((2, 2, 4, NZ, HALF, WB), BF16),
    rbx=((3, 4, NZ, HALF, WB), BF16),
    gb=((4, NZ, HALF, WB), F32),
    gbb=((4, NZ, HALF, WB), BF16),
    rby=((3, NZ, HALF, WB), BF16),
    hb=((NZ, HALF, WB), F32),
    rbz=((7, HALF, WB), F32),
    pc=((4, 2, 2, NZ, HALF, WB), F32),
    pcb=((4, 2, 2, NZ, HALF, WB), BF16),
    rcy=((3, 2, 2, NZ, HALF, WB), BF16),
    gc=((2, 2, NZ, HALF, WB), F32),
    gcb=((2, 2, NZ, HALF, WB), BF16),
    rcx=((3, NZ, HALF, WB), BF16),
    hc=((NZ, HALF, WB), F32),
    rcz=((7, HALF, WB), F32),
    ob=((SPAN, BLOCK), F32),
)
N_REMOTE = 190
N_LOCAL = 16


def main_kernel(queries, passages, dense, entropy, loss, grad_queries, grad_passages, *scratch):
    buf = dict(zip(SCRATCH, scratch))
    send_sems, recv_sems, local_sems = scratch[len(SCRATCH) :]
    qs, ws, tt, lv, st, sr, grid = (buf[k] for k in ("qs", "ws", "tt", "lv", "st", "sr", "grid"))
    go, gs, gr = (buf[k] for k in ("go", "gs", "gr"))
    x, y, z, core = place()
    xh = x // 2
    used = [0, 0]
    sent = []

    def remote(src, dst, target):
        index = used[0]
        used[0] += 1
        copy = pltpu.make_async_remote_copy(
            src_ref=src,
            dst_ref=dst,
            send_sem=send_sems.at[index],
            recv_sem=recv_sems.at[index],
            device_id=target,
            device_id_type=MESH,
        )
        copy.start()
        sent.append(copy)
        return copy

    def local(src, dst):
        index = used[1]
        used[1] += 1
        copy = pltpu.make_async_copy(src, dst, local_sems.at[index])
        copy.start()
        return copy

    sibling = device(x, y, z, 1 - core)
    by_x = {d: device(x + d, y, z, core) for d in (1, 2, 3)}
    by_y = {d: device(x, y + d, z, core) for d in (1, 2, 3)}
    by_z = {d: device(x, y, z + d, core) for d in range(1, NZ)}
    peers = [sibling, *by_x.values(), *by_y.values(), *by_z.values()]

    own_block = local(passages, ws.at[pl.ds(0, SPAN)])
    own_queries = local(queries, qs.at[pl.ds(0, ROWS)])
    own_teacher = local(dense.at[core], tt.at[pl.ds(0, ROWS)])
    barrier = pltpu.get_barrier_semaphore()
    for peer in peers:
        pl.semaphore_signal(barrier, inc=1, device_id=peer, device_id_type=MESH)
    pl.semaphore_wait(barrier, len(peers))

    mine = pl.ds(pl.multiple_of(FLAT + QUARTER * y, LANES), QUARTER)
    flat = pl.ds(0, FLAT)

    def row(dxl, dz):
        return dxl * GROUP + (dz % NZ) * SPAN

    def along_z(dz, way, first=0, count=SPAN):
        target = by_z[1 if way > 0 else NZ - 1]
        here = pl.ds(row(0, dz) + first, count)
        there = pl.ds(row(0, dz - way) + first, count)
        return [remote(ws.at[here, c], ws.at[there, c], target) for c in (mine, flat)]

    def along_x(dz):
        copies = []
        for d, first in ((1, 0), (3, HALF)):
            here = pl.ds(row(0, dz) + first, HALF)
            there = pl.ds(row(1, dz) + first, HALF)
            copies += [remote(ws.at[here, c], ws.at[there, c], by_x[d]) for c in (mine, flat)]
        return copies

    def along_y(dxl, dz):
        here = ws.at[pl.ds(row(dxl, dz), SPAN), mine]
        return [remote(here, here, by_y[d]) for d in (1, 3, 2)]

    def arrived(copies):
        for copy in copies:
            copy.wait_recv()

    own_block.wait()
    x_copies, y_copies = {}, []
    up, down = along_z(0, 1), along_z(0, -1)
    x_copies[0] = along_x(0)
    to_sibling = [
        remote(queries, qs.at[pl.ds(ROWS, ROWS)], sibling),
        remote(dense.at[1 - core], tt.at[pl.ds(ROWS, ROWS)], sibling),
    ]
    for step in (1, 2, 3):
        arrived(up)
        up = along_z(-step, 1, 0, HALF if step == 3 else SPAN)
        x_copies[-step] = along_x(-step)
        y_copies += along_y(0, -step)
        arrived(down)
        if step == 3:
            down = along_z(step, -1, HALF, HALF)
        else:
            down = along_z(step, -1)
        x_copies[step] = along_x(step)
        y_copies += along_y(0, step)
        for dz in {1 - step, step - 1}:
            arrived(x_copies[dz])
            y_copies += along_y(1, dz)
    arrived(up)
    arrived(down)
    x_copies[4] = along_x(4)
    y_copies += along_y(0, 4)
    for dz in (-3, 3, 4):
        arrived(x_copies[dz])
        y_copies += along_y(1, dz)
    own_queries.wait()
    own_teacher.wait()
    arrived(to_sibling)
    arrived(y_copies)

    def dot_rows(a, b):
        return lax.dot_general(a, b, (((1,), (1,)), ((), ())), preferred_element_type=F32)

    column = lax.broadcasted_iota(jnp.int32, (2 * ROWS, W2), 1)
    head = qs[:, 0:W2]
    zero = jnp.zeros_like(head)
    lv[0] = dot_rows(jnp.where(column < W1, head, zero), ws[:, 0:W2])
    lv[1] = lv[0] + dot_rows(jnp.where(column < W1, zero, head), ws[:, 0:W2])
    lv[2] = lv[1] + dot_rows(qs[:, W2:W3], ws[:, W2:W3])
    lv[3] = lv[2]

    def score_step(index, carry):
        cols = pl.ds(pl.multiple_of(index * 1024, 1024), 1024)
        lv[3] += dot_rows(qs[:, cols], ws[:, cols])
        return carry

    lax.fori_loop(1, E // 1024, score_step, 0)

    scales = [1.0 / math.sqrt(width) for width in WIDTHS]
    teacher_or = tt[...]
    chosen = teacher_or >= 0.0
    teacher = jnp.where(chosen, teacher_or, 0.0)
    columns = [None] * 13
    for level in range(4):
        logits = lv[level] * scales[level]
        top = jnp.max(jnp.where(chosen, logits, -BIG), axis=1, keepdims=True)
        shifted = jnp.where(chosen, logits - top, 0.0)
        weight = jnp.where(chosen, jnp.exp(shifted), 0.0)
        lv[level] = weight
        columns[level] = top
        columns[4 + level] = jnp.sum(weight, axis=1, keepdims=True)
        columns[8 + level] = jnp.sum(teacher * shifted, axis=1, keepdims=True)
    columns[12] = jnp.sum(teacher, axis=1, keepdims=True)
    lane = lax.broadcasted_iota(jnp.int32, (2 * ROWS, LANES), 1)
    table = jnp.zeros((2 * ROWS, LANES), F32)
    for index, value in enumerate(columns):
        table = jnp.where(lane == index, value, table)
    st[...] = table
    stats_copy = remote(st, sr, sibling)
    stats_copy.wait_recv()
    received = sr[...]
    other = jnp.concatenate([received[ROWS:], received[:ROWS]], axis=0)
    loss_rows = jnp.zeros((ROWS, 1), F32)
    teacher_sum = (columns[12] + other[:, 12:13])[:ROWS]
    tail = None
    for level in (3, 2, 1, 0):
        top, top_other = columns[level], other[:, level : level + 1]
        peak = jnp.maximum(top, top_other)
        fade, fade_other = jnp.exp(top - peak), jnp.exp(top_other - peak)
        total = columns[4 + level] * fade + other[:, 4 + level : 5 + level] * fade_other
        part = columns[8 + level] + columns[12] * (top - peak)
        part_other = other[:, 8 + level : 9 + level] + other[:, 12:13] * (top_other - peak)
        loss_rows += jnp.log(total[:ROWS]) * teacher_sum - (part + part_other)[:ROWS]
        dlogit = (lv[level] * (fade / total) - teacher) * scales[level]
        tail = dlogit if tail is None else dlogit + tail
        grid[level] = tail.astype(BF16)
    loss[...] = 4.0 * entropy[...] + loss_rows

    pa, pab, pb, pbb, pc, pcb = (buf[k] for k in ("pa", "pab", "pb", "pbb", "pc", "pcb"))

    def dot_columns(a, b):
        return lax.dot_general(a, b, (((0,), (0,)), ((), ())), preferred_element_type=F32)

    def keep(dxl, q, result):
        rounded = result.astype(BF16)
        xh_of, y_of = q // 4, q % 4
        for dz in range(NZ):
            top = slice(dz * SPAN, dz * SPAN + HALF)
            low = slice(dz * SPAN + HALF, (dz + 1) * SPAN)
            whole = slice(dz * SPAN, (dz + 1) * SPAN)
            pa[dz, dxl, q] = result[whole, :WA]
            pab[dz, dxl, q] = rounded[whole, :WA]
            pb[dxl, xh_of, y_of, dz] = result[top, WA:]
            pbb[dxl, xh_of, y_of, dz] = rounded[top, WA:]
            pc[y_of, dxl, xh_of, dz] = result[low, WA:]
            pcb[y_of, dxl, xh_of, dz] = rounded[low, WA:]

    for dxl in range(2):
        part = pl.ds(dxl * GROUP, GROUP)
        narrow = lax.broadcasted_iota(jnp.int32, (GROUP, W2), 1) < W1
        first = qs[:, 0:W2]
        first = jnp.where(
            narrow, dot_columns(grid[0, :, part], first), dot_columns(grid[1, :, part], first)
        )
        second = dot_columns(grid[2, :, part], qs[:, W2:BLOCK])
        keep(dxl, 0, jnp.concatenate([first, second], axis=1))
        keep(dxl, 1, dot_columns(grid[2, :, part], qs[:, BLOCK : 2 * BLOCK]))
        for q in range(2, 8):
            keep(dxl, q, dot_columns(grid[3, :, part], qs[:, q * BLOCK : (q + 1) * BLOCK]))

    ra, rax, ray, fa, ga = (buf[k] for k in ("ra", "rax", "ray", "fa", "ga"))

    def ring(way, step, dxl):
        dz = (way * (5 - step)) % NZ
        target = by_z[1 if way > 0 else NZ - 1]
        slot = ra.at[0 if way > 0 else 1, step - 1, dxl]
        if step == 1:
            rows = pl.ds(0 if way > 0 else HALF, HALF)
            return remote(pab.at[dz, dxl, :, rows], slot.at[:, rows], target)
        return remote(pab.at[dz, dxl], slot, target)

    def toward(d):
        return ((x + d) % NX) // 2

    rings = {(way, dxl): ring(way, 1, dxl) for dxl in range(2) for way in (1, -1)}
    b_copies = [remote(pbb.at[d % 2, toward(d)], buf["rbx"].at[d - 1], by_x[d]) for d in (1, 2, 3)]
    c_copies = [remote(pcb.at[(y + d) % NY], buf["rcy"].at[d - 1], by_y[d]) for d in (1, 2, 3)]

    def dot_plain(a, b):
        return jnp.dot(a, b, preferred_element_type=F32)

    def keep_query(cols, result):
        go[:, cols] = result[:ROWS]
        gs[:, cols] = result[ROWS:]

    first = ws[:, 0:W2]
    keep_query(
        slice(0, W2), jnp.where(column < W1, dot_plain(grid[0], first), dot_plain(grid[1], first))
    )
    keep_query(slice(W2, BLOCK), dot_plain(grid[2], ws[:, W2:BLOCK]))
    keep_query(slice(BLOCK, W3), dot_plain(grid[2], ws[:, BLOCK:W3]))

    def query_step(index, carry):
        cols = pl.ds(pl.multiple_of(index * BLOCK, BLOCK), BLOCK)
        keep_query(cols, dot_plain(grid[3], ws[:, cols]))
        return carry

    lax.fori_loop(2, E // BLOCK, query_step, 0)
    query_copy = remote(gs, gr, sibling)

    for step in (1, 2, 3):
        for dxl in range(2):
            for way in (1, -1):
                rings[way, dxl].wait_recv()
                dz = (way * (4 - step)) % NZ
                slot = ra.at[0 if way > 0 else 1, step - 1, dxl]
                rows = pl.ds(0, SPAN)
                if step == 1:
                    rows = pl.ds(0 if way > 0 else HALF, HALF)
                pab[dz, dxl, :, rows] = (pa[dz, dxl, :, rows] + slot[:, rows].astype(F32)).astype(
                    BF16
                )
                rings[way, dxl] = ring(way, step + 1, dxl)
        if step == 1:
            query_copy.wait_recv()
            go[...] += gr[...]
            out_copy = local(go, grad_queries)
    for dxl in range(2):
        rings[1, dxl].wait_recv()
        rings[-1, dxl].wait_recv()
        total = pa[0, dxl] + ra[0, 3, dxl].astype(F32) + ra[1, 3, dxl].astype(F32)
        fa[dxl] = total.reshape(2, 4, SPAN, WA)
    ax_copies = [remote(fa.at[d % 2, toward(d)], rax.at[d - 1], by_x[d]) for d in (1, 2, 3)]

    gb, gbb, rbx, rby, hb, rbz = (buf[k] for k in ("gb", "gbb", "rbx", "rby", "hb", "rbz"))
    gc, gcb, rcy, rcx, hc, rcz = (buf[k] for k in ("gc", "gcb", "rcy", "rcx", "hc", "rcz"))
    arrived(b_copies)
    total = pb[0, xh] + rbx[0].astype(F32) + rbx[1].astype(F32) + rbx[2].astype(F32)
    gb[...] = total
    gbb[...] = total.astype(BF16)
    b_copies = [remote(gbb.at[(y + d) % NY], rby.at[d - 1], by_y[d]) for d in (1, 2, 3)]
    arrived(c_copies)
    total = pc[y] + rcy[0].astype(F32) + rcy[1].astype(F32) + rcy[2].astype(F32)
    gc[...] = total
    gcb[...] = total.astype(BF16)
    c_copies = [remote(gcb.at[d % 2, toward(d)], rcx.at[d - 1], by_x[d]) for d in (1, 2, 3)]
    arrived(ax_copies)
    ga[...] = fa[0, xh] + rax[0] + rax[1] + rax[2]
    ay_copies = [remote(ga.at[(y + d) % NY], ray.at[d - 1], by_y[d]) for d in (1, 2, 3)]

    arrived(b_copies)
    hb[...] = gb[y] + rby[0].astype(F32) + rby[1].astype(F32) + rby[2].astype(F32)
    bz_copies = [remote(hb.at[d], rbz.at[d - 1], by_z[d]) for d in range(1, NZ)]
    arrived(c_copies)
    hc[...] = gc[0, xh] + rcx[0].astype(F32) + rcx[1].astype(F32) + rcx[2].astype(F32)
    cz_copies = [remote(hc.at[d], rcz.at[d - 1], by_z[d]) for d in range(1, NZ)]
    arrived(ay_copies)
    ob = buf["ob"]
    ob[:, :WA] = ga[y] + ray[0] + ray[1] + ray[2]
    arrived(bz_copies)
    arrived(cz_copies)
    total_b, total_c = hb[0], hc[0]
    for index in range(NZ - 1):
        total_b += rbz[index]
        total_c += rcz[index]
    ob[:HALF, WA:] = total_b
    ob[HALF:, WA:] = total_c
    last = local(ob, grad_passages)
    for copy in sent:
        copy.wait_send()
    out_copy.wait()
    last.wait()


def main_call(queries, passages, dense, entropy):
    scratch = [pltpu.VMEM(shape, dtype) for shape, dtype in SCRATCH.values()]
    scratch += [
        pltpu.SemaphoreType.DMA((N_REMOTE,)),
        pltpu.SemaphoreType.DMA((N_REMOTE,)),
        pltpu.SemaphoreType.DMA((N_LOCAL,)),
    ]
    anywhere = pl.BlockSpec(memory_space=pl.ANY)
    return pl.pallas_call(
        main_kernel,
        out_shape=(
            jax.ShapeDtypeStruct((ROWS, LANES), F32),
            jax.ShapeDtypeStruct((ROWS, E), F32),
            jax.ShapeDtypeStruct((SPAN, BLOCK), F32),
        ),
        in_specs=[anywhere, anywhere, anywhere, pl.BlockSpec(memory_space=pltpu.VMEM)],
        out_specs=(pl.BlockSpec(memory_space=pltpu.VMEM), anywhere, anywhere),
        scratch_shapes=scratch,
        compiler_params=pltpu.CompilerParams(
            collective_id=0, has_side_effects=True, vmem_limit_bytes=60 * 2**20
        ),
        name="distill",
    )(queries, passages, dense, entropy)


def shards(queries, passages, candidates, teacher_scores):
    dense, entropy = prepare(candidates, teacher_scores)
    loss, grad_queries, grad_passages = main_call(queries, passages, dense, entropy)
    return (loss[:, 0], grad_queries, grad_passages)


def solution(mesh):
    return jax.shard_map(
        shards,
        mesh=mesh,
        in_specs=(
            P(("query", "passage"), None),
            P("passage", None),
            P(("query", "passage"), None),
            P(("query", "passage"), None),
        ),
        out_specs=(P(("query", "passage")), P(("query", "passage"), None), P("passage", "query")),
        check_vma=False,
    )
```

time: 1180 us -> 101 us (0.09)
  local copies, waits for them, and re-layouts: 792 us -> 5.24 us
  waiting for transfers between devices: 322 us -> 0 us
  Pallas kernels: 0 us -> 95 us
  matrix products: 27.4 us -> 0 us
  other arithmetic: 15.3 us -> 0 us
  between operations: 14.5 us -> 0.64 us
    gather x4 -> x0, local copies, waits for them, and re-layouts: 518 us -> none  [piece_logits(): picked.append(jnp.take_along_axis(running, clipped, axis=1))]
    reduce_scatter x2 -> x0, waiting for transfers between devices: 257 us -> none  [the longest x1 189 us: shards(): lax.psum_scatter(passage_term(flipped, query_parts), 'passage', scatter_d...]
    unnamed x22 -> x4, local copies, waits for them, and re-layouts: 168 us -> 3.78 us
    pallas_call x0 -> x2, Pallas kernels: none -> 95 us  [the longest x1 89.2 us: main_call(): pl.pallas_call(main_kernel, out_shape=(jax.ShapeDtypeStruct((ROWS, LANES)...]
    slice x2 -> x1, local copies, waits for them, and re-layouts: 81.9 us -> 1.47 us  [shards(): return (loss[:, 0], grad_queries, grad_passages)]
    all_gather x1 -> x0, waiting for transfers between devices: 64.2 us -> none  [shards(): passage_pool = lax.all_gather(passages, 'passage', axis=0, tiled=True)]
    dot_general x12 -> x0, matrix products: 27.4 us -> none  [the longest x4 9.74 us: piece_logits(): jnp.einsum('qd,pd->qp', query_parts[segment], shard_parts[segment], prefe...]
    concatenate x2 -> x0, local copies, waits for them, and re-layouts: 20.3 us -> none  [the longest x1 18.2 us: passage_term(): return jnp.concatenate(products, axis=1)]
  transfers between devices with their start and end apart: 3 -> 0, of which waited for: 3 -> 0; matrix products, arithmetic and copies ran while one was open for 2% -> 0% of each run, Pallas kernels for 0% -> 0%
where the time goes in v1:
time: 101 us
  Pallas kernels  95 us (94%)
  local copies, waits for them, and re-layouts  5.24 us (5%)
    pallas_call x1, Pallas kernels, main_call(): pl.pallas_call(main_kernel, out_shape=(jax.ShapeDtypeStruct((ROWS, LANES)...  89.2 us
    pallas_call x1, Pallas kernels, prepare(): pl.pallas_call(prep_kernel, out_shape=(jax.ShapeDtypeStruct((2, ROWS, POO...  5.8 us
    unnamed x4, local copies, waits for them, and re-layouts  3.78 us

profile of v1, /device:TPU:1, one launch (start us, length us, event | category | flops | bytes accessed | tf_op | source)
XLA Modules:
  0.0 100.9 jit_solution(4798973942683768615)
XLA Ops:
  0.6 5.8 %prepare.1 = (f32[2,128,512]{2,1,0:T(8,128)}, f32[128,128]{1,0:T(8,128)}) custom-call(s32[128,128]{1,0:T(8,128)} %candidates.1, f32[128,128]{1,0:T(8,128)} %scores.1), custom_call_target="tpu_custom_call" | custom-call | tf_op jit(solution)/shard_map/prepare/pallas_call | solution.py:74
  6.4 89.2 %distill.1 = (f32[128,128]{1,0:T(8,128)}, f32[128,4096]{1,0:T(8,128)}, f32[32,512]{1,0:T(8,128)}) custom-call(bf16[128,4096]{1,0:T(8,128)(2,1)} %queries.1, bf16[32,4096]{1,0:T(8,128)(2,1)} %passages.1, f32[2,128,512]{2,1,0:T(8,128)} %get-tuple-element.8.dense, f32[128,128]{1,0:T(8,128)} %get-tuple-element.9.entropy), custom_call_target="tpu_custom_call" | custom-call | tf_op jit(solution)/shard_map/distill/pallas_call | solution.py:437
  95.6 1.5 %slice_reduce_fusion = f32[128]{0:T(128)} fusion(f32[128,128]{1,0:T(8,128)} %get-tuple-element.10), kind=kLoop, calls=%fused_computation | loop fusion | bytes 1024 | tf_op jit(solution)/shard_map/slice | solution.py:457
  97.1 0.0 copy-start
  97.1 3.1 %copy.9 = f32[128,4096]{1,0:T(8,128)} copy(f32[128,4096]{1,0:T(8,128)} %get-tuple-element.17) | data formatting | bytes 4194304
  100.2 0.0 copy-done
  100.3 0.6 copy.10
Async XLA Ops:
  97.1 3.1 %copy-start = (f32[32,512]{1,0:T(8,128)S(1)}, f32[32,512]{1,0:T(8,128)}, u32[]{:S(2)}) copy-start(f32[32,512]{1,0:T(8,128)} %get-tuple-element.18) | copy-start | bytes 196612

commit v2 on v1

v2 whole, which is shorter than its diff:
```python
import functools
import math

import jax
import jax.numpy as jnp
from jax import lax
from jax.experimental import pallas as pl
from jax.experimental.pallas import tpu as pltpu
from jax.sharding import PartitionSpec as P

MESH = pl.DeviceIdType.MESH
BF16 = jnp.bfloat16
F32 = jnp.float32

E = 4096
W1, W2, W3 = 64, 256, 1024
WIDTHS = (W1, W2, W3, E)
ROWS = 128
SPAN = 32
HALF = 16
NX, NY, NZ = 4, 4, 8
POOL = 2 * NZ * SPAN
GROUP = NZ * SPAN
LANES = 128
BIG = 3.0e38

QUARTER = 384
FLAT = E - 4 * QUARTER
PIECES = 2
GATHER_ORDER = (
    ('m', 1), ('x', 0), (0, 1), (1, 1), ('m', 2), ('x', 1), (0, 2), (1, 2), ('m', 3), ('x', 2), (0, 3), (1, 3), ('m', 4), ('x', 3), (0, 4), (1, 4), ('x', 4)
)

BLOCK = 512
WA = 128
WB = BLOCK - WA
FIRST_Z = 2
CHUNKS = ((0, 5), (5, 3))


def place():
    query = lax.axis_index("query")
    passage = lax.axis_index("passage")
    x = (query // 4) * 2 + (passage // 2) % 2
    return x, query % 4, passage // 4, passage % 2


def device(x, y, z, core):
    x, y, z = x % NX, y % NY, z % NZ
    return ((x // 2) * 4 + y, (z * 2 + x % 2) * 2 + core)


SCRATCH = dict(
    qs=((2 * ROWS, E), BF16),
    ws=((2 * GROUP, E), BF16),
    cs=((2 * ROWS, LANES), jnp.int32),
    rs=((2 * ROWS, LANES), F32),
    ts=((2 * ROWS, LANES), F32),
    tt=((2 * ROWS, POOL), F32),
    lv=((4, 2 * ROWS, POOL), F32),
    st=((2 * ROWS, LANES), F32),
    sr=((2 * ROWS, LANES), F32),
    grid=((4, 2 * ROWS, POOL), BF16),
    go=((ROWS, E), F32),
    gs=((ROWS, E), F32),
    gr=((ROWS, E), F32),
    pa=((NZ, 2, 8, SPAN, WA), F32),
    pab=((NZ, 2, 8, SPAN, WA), BF16),
    ra=((2, 4, 2, 8, SPAN, WA), BF16),
    fa=((2, 2, 4, SPAN, WA), F32),
    rax=((3, 4, SPAN, WA), F32),
    ga=((4, SPAN, WA), F32),
    ray=((3, SPAN, WA), F32),
    pb=((2, 2, 4, NZ, HALF, WB), F32),
    pbb=((2, 2, 4, NZ, HALF, WB), BF16),
    rbx=((3, 4, NZ, HALF, WB), BF16),
    gb=((4, NZ, HALF, WB), F32),
    gbb=((4, NZ, HALF, WB), BF16),
    rby=((3, NZ, HALF, WB), BF16),
    hb=((NZ, HALF, WB), F32),
    hbb=((NZ, HALF, WB), BF16),
    rbz=((NZ, HALF, WB), F32),
    rbzb=((NZ, HALF, WB), BF16),
    pc=((4, 2, 2, NZ, HALF, WB), F32),
    pcb=((4, 2, 2, NZ, HALF, WB), BF16),
    rcy=((3, 2, 2, NZ, HALF, WB), BF16),
    gc=((2, 2, NZ, HALF, WB), F32),
    gcb=((2, 2, NZ, HALF, WB), BF16),
    rcx=((3, NZ, HALF, WB), BF16),
    hc=((NZ, HALF, WB), F32),
    hcb=((NZ, HALF, WB), BF16),
    rcz=((NZ, HALF, WB), F32),
    rczb=((NZ, HALF, WB), BF16),
    ob=((SPAN, BLOCK), F32),
)
N_REMOTE = 260
N_LOCAL = 16


def main_kernel(queries, passages, candidates, scores, loss, grad_queries, grad_passages, *scratch):
    buf = dict(zip(SCRATCH, scratch))
    send_sems, recv_sems, local_sems = scratch[len(SCRATCH) :]
    qs, ws, tt, lv, st, sr, grid = (buf[k] for k in ("qs", "ws", "tt", "lv", "st", "sr", "grid"))
    go, gs, gr = (buf[k] for k in ("go", "gs", "gr"))
    x, y, z, core = place()
    xh = x // 2
    used = [0, 0]
    sent = []

    def remote(src, dst, target):
        index = used[0]
        used[0] += 1
        copy = pltpu.make_async_remote_copy(
            src_ref=src,
            dst_ref=dst,
            send_sem=send_sems.at[index],
            recv_sem=recv_sems.at[index],
            device_id=target,
            device_id_type=MESH,
        )
        copy.start()
        sent.append(copy)
        return copy

    def local(src, dst):
        index = used[1]
        used[1] += 1
        copy = pltpu.make_async_copy(src, dst, local_sems.at[index])
        copy.start()
        return copy

    sibling = device(x, y, z, 1 - core)
    by_x = {d: device(x + d, y, z, core) for d in (1, 2, 3)}
    by_y = {d: device(x, y + d, z, core) for d in (1, 2, 3)}
    by_z = {d: device(x, y, z + d, core) for d in range(1, NZ)}
    peers = [sibling, *by_x.values(), *by_y.values(), *by_z.values()]

    own_block = local(passages, ws.at[pl.ds(0, SPAN)])
    own_queries = local(queries, qs.at[pl.ds(0, ROWS)])
    own_teacher = [
        local(candidates, buf["cs"].at[pl.ds(0, ROWS)]),
        local(scores, buf["rs"].at[pl.ds(0, ROWS)]),
    ]
    barrier = pltpu.get_barrier_semaphore()
    for peer in peers:
        pl.semaphore_signal(barrier, inc=1, device_id=peer, device_id_type=MESH)
    pl.semaphore_wait(barrier, len(peers))

    mine = pl.ds(pl.multiple_of(FLAT + QUARTER * y, LANES), QUARTER)
    pieces = {"m": mine}
    for index in range(PIECES):
        pieces[index] = pl.ds(index * (FLAT // PIECES), FLAT // PIECES)

    def row(dxl, dz):
        return dxl * GROUP + (dz % NZ) * SPAN

    z_copies, x_copies, y_copies = {}, {}, ([], [])

    def along_z(piece, step, way):
        dz, cols = -way * step, pieces[piece]
        first, count = (0 if way > 0 else HALF, HALF) if step == 3 else (0, SPAN)
        here = pl.ds(row(0, dz) + first, count)
        there = pl.ds(row(0, dz - way) + first, count)
        target = by_z[1 if way > 0 else NZ - 1]
        z_copies[piece, step + 1, way] = remote(ws.at[here, cols], ws.at[there, cols], target)

    def along_x(piece, dz):
        cols = pieces[piece]
        copies = []
        for d, first in ((1, 0), (3, HALF)):
            here = pl.ds(row(0, dz) + first, HALF)
            there = pl.ds(row(1, dz) + first, HALF)
            copies.append(remote(ws.at[here, cols], ws.at[there, cols], by_x[d]))
        x_copies[piece, dz] = copies

    def along_y(dxl, dz):
        here = ws.at[pl.ds(row(dxl, dz), SPAN), mine]
        for d in (1, 3, 2):
            y_copies[dxl].append(remote(here, here, by_y[d]))

    def arrived_here(copies):
        for copy in copies:
            copy.wait()

    def arrived(copies):
        for copy in copies:
            copy.wait_recv()

    own_block.wait()
    for piece in ('m', 0, 1):
        for way in (1, -1):
            along_z(piece, 0, way)
        along_x(piece, 0)
    to_sibling = [
        remote(candidates, buf["cs"].at[pl.ds(ROWS, ROWS)], sibling),
        remote(scores, buf["rs"].at[pl.ds(ROWS, ROWS)], sibling),
        remote(queries, qs.at[pl.ds(ROWS, ROWS)], sibling),
    ]
    x_done = set()

    def from_x(piece, dz):
        arrived(x_copies[piece, dz])
        x_done.add((piece, dz))
        if piece == "m":
            along_y(1, dz)

    cs, rs, ts = buf["cs"], buf["rs"], buf["ts"]
    lane = lax.broadcasted_iota(jnp.int32, (ROWS, LANES), 1)
    entropy = []

    def teach(rows):
        raw = rs[rows]
        shifted = raw - jnp.max(raw, axis=1, keepdims=True)
        log_teacher = shifted - jnp.log(jnp.sum(jnp.exp(shifted), axis=1, keepdims=True))
        value = jnp.exp(log_teacher)
        ts[rows] = value
        entropy.append(jnp.sum(value * log_teacher, axis=1, keepdims=True))

    def spread(rows, chunk):
        chosen = cs[rows]
        slot = lane // SPAN + chunk * (LANES // SPAN)
        dxl, dz = slot // NZ, slot % NZ
        owner = (((z + dz) % NZ) * 2 + (x + dxl) % 2) * 2 + core
        target = owner * SPAN + lane % SPAN
        position = jnp.zeros((ROWS, LANES), jnp.int32)
        for step in (64, 32, 16, 8, 4, 2, 1):
            probe = jnp.take_along_axis(chosen, position + (step - 1), axis=1)
            position = jnp.where(probe < target, position + step, position)
        hit = jnp.take_along_axis(chosen, position, axis=1) == target
        value = jnp.take_along_axis(ts[rows], position, axis=1)
        tt[rows, chunk * LANES : (chunk + 1) * LANES] = jnp.where(hit, value, -1.0)

    own, other = pl.ds(0, ROWS), pl.ds(ROWS, ROWS)
    chores = [lambda: (arrived_here(own_teacher), teach(own))]
    chores += [lambda chunk=chunk: spread(own, chunk) for chunk in range(POOL // LANES)]
    chores += [lambda: (arrived(to_sibling[:2]), teach(other))]
    chores += [lambda chunk=chunk: spread(other, chunk) for chunk in range(POOL // LANES)]

    for piece, step in GATHER_ORDER:
        if piece == "x":
            for dz in ((0,) if step == 0 else (4,) if step == 4 else (-step, step)):
                from_x("m", dz)
            continue
        for way in (1, -1):
            z_copies[piece, step, way].wait_recv()
            if step < 4:
                along_z(piece, step, way)
                along_x(piece, -way * step)
                if piece == "m":
                    along_y(0, -way * step)
        if step == 4:
            along_x(piece, 4)
            if piece == "m":
                along_y(0, 4)
        if chores and (piece, step) != ("m", 1):
            chores.pop(0)()
    for chore in chores:
        chore()
    def dot_rows(a, b):
        return lax.dot_general(a, b, (((1,), (1,)), ((), ())), preferred_element_type=F32)

    column = lax.broadcasted_iota(jnp.int32, (2 * ROWS, W2), 1)
    own_queries.wait()
    arrived(to_sibling[2:])
    for dxl in range(2):
        if dxl == 1:
            for key in x_copies:
                if key not in x_done:
                    from_x(*key)
        arrived(y_copies[dxl])
        if dxl == 1:
            pass
        rows = pl.ds(dxl * GROUP, GROUP)
        head = qs[:, 0:W2]
        zero = jnp.zeros_like(head)
        narrow = ws[rows, 0:W2]
        level = dot_rows(jnp.where(column < W1, head, zero), narrow)
        lv[0, :, rows] = level
        level += dot_rows(jnp.where(column < W1, zero, head), narrow)
        lv[1, :, rows] = level
        level += dot_rows(qs[:, W2:W3], ws[rows, W2:W3])
        lv[2, :, rows] = level

        def score_step(index, total, rows=rows):
            cols = pl.ds(pl.multiple_of(index * 1024, 1024), 1024)
            return total + dot_rows(qs[:, cols], ws[rows, cols])

        lv[3, :, rows] = lax.fori_loop(1, E // 1024, score_step, level)


    scales = [1.0 / math.sqrt(width) for width in WIDTHS]
    teacher_or = tt[...]
    chosen = teacher_or >= 0.0
    teacher = jnp.where(chosen, teacher_or, 0.0)
    columns = [None] * 13
    for level in range(4):
        logits = lv[level] * scales[level]
        top = jnp.max(jnp.where(chosen, logits, -BIG), axis=1, keepdims=True)
        shifted = jnp.where(chosen, logits - top, 0.0)
        weight = jnp.where(chosen, jnp.exp(shifted), 0.0)
        lv[level] = weight
        columns[level] = top
        columns[4 + level] = jnp.sum(weight, axis=1, keepdims=True)
        columns[8 + level] = jnp.sum(teacher * shifted, axis=1, keepdims=True)
    columns[12] = jnp.sum(teacher, axis=1, keepdims=True)
    place_of = lax.broadcasted_iota(jnp.int32, (2 * ROWS, LANES), 1)
    table = jnp.zeros((2 * ROWS, LANES), F32)
    for index, value in enumerate(columns):
        table = jnp.where(place_of == index, value, table)
    st[...] = table
    stats_copy = remote(st, sr, sibling)
    stats_copy.wait_recv()
    received = sr[...]
    swapped = jnp.concatenate([received[ROWS:], received[:ROWS]], axis=0)
    loss_rows = jnp.zeros((ROWS, 1), F32)
    teacher_sum = (columns[12] + swapped[:, 12:13])[:ROWS]
    tail = None
    for level in (3, 2, 1, 0):
        top, top_other = columns[level], swapped[:, level : level + 1]
        peak = jnp.maximum(top, top_other)
        fade, fade_other = jnp.exp(top - peak), jnp.exp(top_other - peak)
        total = columns[4 + level] * fade + swapped[:, 4 + level : 5 + level] * fade_other
        part = columns[8 + level] + columns[12] * (top - peak)
        part_other = swapped[:, 8 + level : 9 + level] + swapped[:, 12:13] * (top_other - peak)
        loss_rows += jnp.log(total[:ROWS]) * teacher_sum - (part + part_other)[:ROWS]
        dlogit = (lv[level] * (fade / total) - teacher) * scales[level]
        tail = dlogit if tail is None else dlogit + tail
        grid[level] = tail.astype(BF16)
    diagonal = lax.broadcasted_iota(jnp.int32, (ROWS, LANES), 0) == lax.broadcasted_iota(
        jnp.int32, (ROWS, LANES), 1
    )
    loss_rows += 4.0 * entropy[0]
    loss[...] = jnp.sum(jnp.where(diagonal, loss_rows, 0.0), axis=0, keepdims=True)


    pa, pab, pb, pbb, pc, pcb = (buf[k] for k in ("pa", "pab", "pb", "pbb", "pc", "pcb"))

    def dot_columns(a, b):
        return lax.dot_general(a, b, (((0,), (0,)), ((), ())), preferred_element_type=F32)

    def keep(dxl, q, result):
        rounded = result.astype(BF16)
        xh_of, y_of = q // 4, q % 4
        for dz in range(NZ):
            top = slice(dz * SPAN, dz * SPAN + HALF)
            low = slice(dz * SPAN + HALF, (dz + 1) * SPAN)
            whole = slice(dz * SPAN, (dz + 1) * SPAN)
            pa[dz, dxl, q] = result[whole, :WA]
            pab[dz, dxl, q] = rounded[whole, :WA]
            at = (dz - FIRST_Z) % NZ
            pb[dxl, xh_of, y_of, at] = result[top, WA:]
            pbb[dxl, xh_of, y_of, at] = rounded[top, WA:]
            pc[y_of, dxl, xh_of, at] = result[low, WA:]
            pcb[y_of, dxl, xh_of, at] = rounded[low, WA:]

    for dxl in range(2):
        part = pl.ds(dxl * GROUP, GROUP)
        narrow = lax.broadcasted_iota(jnp.int32, (GROUP, W2), 1) < W1
        first = qs[:, 0:W2]
        first = jnp.where(
            narrow, dot_columns(grid[0, :, part], first), dot_columns(grid[1, :, part], first)
        )
        second = dot_columns(grid[2, :, part], qs[:, W2:BLOCK])
        keep(dxl, 0, jnp.concatenate([first, second], axis=1))
        keep(dxl, 1, dot_columns(grid[2, :, part], qs[:, BLOCK : 2 * BLOCK]))
        for q in range(2, 8):
            keep(dxl, q, dot_columns(grid[3, :, part], qs[:, q * BLOCK : (q + 1) * BLOCK]))


    ra, rax, ray, fa, ga = (buf[k] for k in ("ra", "rax", "ray", "fa", "ga"))

    def ring(way, step, dxl):
        dz = (way * (5 - step)) % NZ
        target = by_z[1 if way > 0 else NZ - 1]
        slot = ra.at[0 if way > 0 else 1, step - 1, dxl]
        if step == 1:
            rows = pl.ds(0 if way > 0 else HALF, HALF)
            return remote(pab.at[dz, dxl, :, rows], slot.at[:, rows], target)
        return remote(pab.at[dz, dxl], slot, target)

    def toward(d):
        return ((x + d) % NX) // 2

    rings = {(way, dxl): ring(way, 1, dxl) for dxl in range(2) for way in (1, -1)}
    gb, gbb, rbx, rby = (buf[k] for k in ("gb", "gbb", "rbx", "rby"))
    gc, gcb, rcy, rcx = (buf[k] for k in ("gc", "gcb", "rcy", "rcx"))
    b_copies, c_copies = [], []
    for start, count in CHUNKS:
        part = pl.ds(start, count)
        b_copies.append(
            [
                remote(pbb.at[d % 2, toward(d), :, part], rbx.at[d - 1, :, part], by_x[d])
                for d in (2, 1, 3)
            ]
        )
        c_copies.append(
            [
                remote(pcb.at[(y + d) % NY, :, :, part], rcy.at[d - 1, :, :, part], by_y[d])
                for d in (2, 1, 3)
            ]
        )

    def dot_plain(a, b):
        return jnp.dot(a, b, preferred_element_type=F32)

    def keep_query(cols, result):
        go[:, cols] = result[:ROWS]
        gs[:, cols] = result[ROWS:]

    first = ws[:, 0:W2]
    keep_query(
        slice(0, W2), jnp.where(column < W1, dot_plain(grid[0], first), dot_plain(grid[1], first))
    )
    keep_query(slice(W2, BLOCK), dot_plain(grid[2], ws[:, W2:BLOCK]))
    keep_query(slice(BLOCK, W3), dot_plain(grid[2], ws[:, BLOCK:W3]))

    def query_step(index, carry):
        cols = pl.ds(pl.multiple_of(index * BLOCK, BLOCK), BLOCK)
        keep_query(cols, dot_plain(grid[3], ws[:, cols]))
        return carry

    lax.fori_loop(2, E // BLOCK, query_step, 0)
    query_copy = remote(gs, gr, sibling)

    def ring_step(step):
        for dxl in range(2):
            for way in (1, -1):
                rings[way, dxl].wait_recv()
                dz = (way * (4 - step)) % NZ
                slot = ra.at[0 if way > 0 else 1, step - 1, dxl]
                rows = pl.ds(0, SPAN)
                if step == 1:
                    rows = pl.ds(0 if way > 0 else HALF, HALF)
                pab[dz, dxl, :, rows] = (pa[dz, dxl, :, rows] + slot[:, rows].astype(F32)).astype(
                    BF16
                )
                rings[way, dxl] = ring(way, step + 1, dxl)

    def ring_end():
        for dxl in range(2):
            rings[1, dxl].wait_recv()
            rings[-1, dxl].wait_recv()
            total = pa[0, dxl] + ra[0, 3, dxl].astype(F32) + ra[1, 3, dxl].astype(F32)
            fa[dxl] = total.reshape(2, 4, SPAN, WA)
        return [remote(fa.at[d % 2, toward(d)], rax.at[d - 1], by_x[d]) for d in (1, 2, 3)]

    def three(own, parts):
        return own + parts[0].astype(F32) + parts[1].astype(F32) + parts[2].astype(F32)

    def b_second(chunk):
        part = pl.ds(*CHUNKS[chunk])
        arrived(b_copies[chunk])
        total = three(pb[0, xh, :, part], rbx[:, :, part])
        gb[:, part] = total
        gbb[:, part] = total.astype(BF16)
        return [
            remote(gbb.at[(y + d) % NY, part], rby.at[d - 1, part], by_y[d]) for d in (2, 1, 3)
        ]

    def c_second(chunk):
        part = pl.ds(*CHUNKS[chunk])
        arrived(c_copies[chunk])
        total = three(pc[y, :, :, part], rcy[:, :, :, part])
        gc[:, :, part] = total
        gcb[:, :, part] = total.astype(BF16)
        return [
            remote(gcb.at[d % 2, toward(d), part], rcx.at[d - 1, part], by_x[d]) for d in (2, 1, 3)
        ]

    def third(chunk, total, wide, narrow, wide_in, narrow_in):
        start, count = CHUNKS[chunk]
        wide[pl.ds(start, count)] = total
        narrow[pl.ds(start, count)] = total.astype(BF16)
        copies = []
        for at in range(start, start + count):
            dz = (at + FIRST_Z) % NZ
            if dz and chunk == 0:
                copies.append(remote(narrow.at[at], narrow_in.at[at], by_z[dz]))
            elif dz:
                copies.append(remote(wide.at[at], wide_in.at[at], by_z[dz]))
        return copies

    hb, hbb, rbz, rbzb = (buf[k] for k in ("hb", "hbb", "rbz", "rbzb"))
    hc, hcb, rcz, rczb = (buf[k] for k in ("hc", "hcb", "rcz", "rczb"))

    def b_third(chunk):
        part = pl.ds(*CHUNKS[chunk])
        arrived(b_next[chunk])
        return third(chunk, three(gb[y, part], rby[:, part]), hb, hbb, rbz, rbzb)

    def c_third(chunk):
        part = pl.ds(*CHUNKS[chunk])
        arrived(c_next[chunk])
        return third(chunk, three(gc[0, xh, part], rcx[:, part]), hc, hcb, rcz, rczb)

    ring_step(1)
    ring_step(2)
    query_copy.wait_recv()
    go[...] += gr[...]
    out_copy = local(go, grad_queries)
    ring_step(3)
    b_next, c_next, last_copies = [None, None], [None, None], []
    b_next[0] = b_second(0)
    c_next[0] = c_second(0)
    ax_copies = ring_end()
    last_copies += b_third(0)
    last_copies += c_third(0)
    b_next[1] = b_second(1)
    c_next[1] = c_second(1)
    arrived(ax_copies)
    ga[...] = three(fa[0, xh], rax)
    ay_copies = [remote(ga.at[(y + d) % NY], ray.at[d - 1], by_y[d]) for d in (1, 2, 3)]
    last_copies += b_third(1)
    last_copies += c_third(1)
    arrived(ay_copies)
    ob = buf["ob"]
    ob[:, :WA] = three(ga[y], ray)
    arrived(last_copies)
    at_home = (0 - FIRST_Z) % NZ
    total_b, total_c = hb[at_home], hc[at_home]
    for at in range(NZ):
        if at < CHUNKS[0][1]:
            total_b += rbzb[at].astype(F32)
            total_c += rczb[at].astype(F32)
        elif at != at_home:
            total_b += rbz[at]
            total_c += rcz[at]
    ob[:HALF, WA:] = total_b
    ob[HALF:, WA:] = total_c
    last = local(ob, grad_passages)
    for copy in sent:
        copy.wait_send()
    out_copy.wait()
    last.wait()


def main_call(queries, passages, candidates, scores):
    scratch = [pltpu.VMEM(shape, dtype) for shape, dtype in SCRATCH.values()]
    scratch += [
        pltpu.SemaphoreType.DMA((N_REMOTE,)),
        pltpu.SemaphoreType.DMA((N_REMOTE,)),
        pltpu.SemaphoreType.DMA((N_LOCAL,)),
    ]
    anywhere = pl.BlockSpec(memory_space=pl.ANY)
    return pl.pallas_call(
        main_kernel,
        out_shape=(
            jax.ShapeDtypeStruct((1, ROWS), F32),
            jax.ShapeDtypeStruct((ROWS, E), F32),
            jax.ShapeDtypeStruct((SPAN, BLOCK), F32),
        ),
        in_specs=[anywhere] * 4,
        out_specs=(pl.BlockSpec(memory_space=pltpu.VMEM), anywhere, anywhere),
        scratch_shapes=scratch,
        compiler_params=pltpu.CompilerParams(
            collective_id=0, has_side_effects=True, vmem_limit_bytes=60 * 2**20
        ),
        name="distill",
    )(queries, passages, candidates, scores)


def shards(queries, passages, candidates, teacher_scores):
    loss, grad_queries, grad_passages = main_call(queries, passages, candidates, teacher_scores)
    return (loss.reshape(ROWS), grad_queries, grad_passages)


def solution(mesh):
    return jax.shard_map(
        shards,
        mesh=mesh,
        in_specs=(
            P(("query", "passage"), None),
            P("passage", None),
            P(("query", "passage"), None),
            P(("query", "passage"), None),
        ),
        out_specs=(P(("query", "passage")), P(("query", "passage"), None), P("passage", "query")),
        check_vma=False,
    )
```

time: 101 us -> 80.8 us (0.80)
  Pallas kernels: 95 us -> 75.2 us
    pallas_call x2 -> x1, Pallas kernels: 95 us -> 75.2 us  [main_call(): pl.pallas_call(main_kernel, out_shape=(jax.ShapeDtypeStruct((1, ROWS), F3...]
    slice x1 -> x0, local copies, waits for them, and re-layouts: 1.47 us -> none  [shards(): return (loss[:, 0], grad_queries, grad_passages)]
    unnamed x4 -> x5, local copies, waits for them, and re-layouts: 3.78 us -> 4.89 us
where the time goes in v2:
time: 80.8 us; the launch traced here: 80.7 us
  Pallas kernels  75.2 us (93%)
  local copies, waits for them, and re-layouts  4.89 us (6%)
    pallas_call x1, Pallas kernels, main_call(): pl.pallas_call(main_kernel, out_shape=(jax.ShapeDtypeStruct((1, ROWS), F3...  75.2 us
    unnamed x5, local copies, waits for them, and re-layouts  4.89 us

profile of v2, /device:TPU:1, one launch (start us, length us, event | category | flops | bytes accessed | tf_op | source)
XLA Modules:
  0.0 80.7 jit_solution(7953723559289797440)
XLA Ops:
  0.6 75.2 %distill.1 = (f32[1,128]{1,0:T(1,128)}, f32[128,4096]{1,0:T(8,128)}, f32[32,512]{1,0:T(8,128)}) custom-call(bf16[128,4096]{1,0:T(8,128)(2,1)} %queries.1, bf16[32,4096]{1,0:T(8,128)(2,1)} %passages.1, s32[128,128]{1,0:T(8,128)} %candidates.1, f32[128,128]{1,0:T(8,128)} %scores.1), custom_call_target="tpu_custom_call" | custom-call | tf_op jit(solution)/shard_map/distill/pallas_call | solution.py:545
  75.8 1.1 %copy.10 = f32[128]{0:T(128)} copy(f32[128]{0:T(128)} %bitcast.1) | data formatting | bytes 1024
  76.9 0.0 copy-start
  76.9 3.1 %copy.11 = f32[128,4096]{1,0:T(8,128)} copy(f32[128,4096]{1,0:T(8,128)} %get-tuple-element.13) | data formatting | bytes 4194304
  80.0 0.0 copy-done
  80.1 0.6 copy.12
Async XLA Ops:
  76.9 3.1 %copy-start = (f32[32,512]{1,0:T(8,128)S(1)}, f32[32,512]{1,0:T(8,128)}, u32[]{:S(2)}) copy-start(f32[32,512]{1,0:T(8,128)} %get-tuple-element.14) | copy-start | bytes 196612

commit v3 on v2

--- a/solution.py
+++ b/solution.py
@@ -23,6 +23,8 @@
 GROUP = NZ * SPAN
 LANES = 128
 BIG = 3.0e38
+PIECE = 16
+STRIP = 32
 
 QUARTER = 384
 FLAT = E - 4 * QUARTER
@@ -36,6 +38,7 @@
 WB = BLOCK - WA
 FIRST_Z = 2
 CHUNKS = ((0, 5), (5, 3))
+FAR = (3, 4, 5)
 
 
 def place():
@@ -58,8 +61,8 @@
     ts=((2 * ROWS, LANES), F32),
     tt=((2 * ROWS, POOL), F32),
     lv=((4, 2 * ROWS, POOL), F32),
-    st=((2 * ROWS, LANES), F32),
-    sr=((2 * ROWS, LANES), F32),
+    st=((3, 2 * ROWS, LANES), F32),
+    sr=((3, 2 * ROWS, LANES), F32),
     grid=((4, 2 * ROWS, POOL), BF16),
     go=((ROWS, E), F32),
     gs=((ROWS, E), F32),
@@ -73,7 +76,8 @@
     ray=((3, SPAN, WA), F32),
     pb=((2, 2, 4, NZ, HALF, WB), F32),
     pbb=((2, 2, 4, NZ, HALF, WB), BF16),
-    rbx=((3, 4, NZ, HALF, WB), BF16),
+    rbr=((2, 2, NZ, HALF, WB), BF16),
+    rbx=((2, 4, NZ, HALF, WB), BF16),
     gb=((4, NZ, HALF, WB), F32),
     gbb=((4, NZ, HALF, WB), BF16),
     rby=((3, NZ, HALF, WB), BF16),
@@ -83,7 +87,8 @@
     rbzb=((NZ, HALF, WB), BF16),
     pc=((4, 2, 2, NZ, HALF, WB), F32),
     pcb=((4, 2, 2, NZ, HALF, WB), BF16),
-    rcy=((3, 2, 2, NZ, HALF, WB), BF16),
+    rcr=((2, 2, NZ, HALF, WB), BF16),
+    rcy=((2, 2, 2, NZ, HALF, WB), BF16),
     gc=((2, 2, NZ, HALF, WB), F32),
     gcb=((2, 2, NZ, HALF, WB), BF16),
     rcx=((3, NZ, HALF, WB), BF16),
@@ -133,7 +138,7 @@
     by_x = {d: device(x + d, y, z, core) for d in (1, 2, 3)}
     by_y = {d: device(x, y + d, z, core) for d in (1, 2, 3)}
     by_z = {d: device(x, y, z + d, core) for d in range(1, NZ)}
-    peers = [sibling, *by_x.values(), *by_y.values(), *by_z.values()]
+    peers = [sibling, *by_x.values(), *by_y.values(), by_z[1], by_z[NZ - 1]]
 
     own_block = local(passages, ws.at[pl.ds(0, SPAN)])
     own_queries = local(queries, qs.at[pl.ds(0, ROWS)])
@@ -289,48 +294,68 @@
 
 
     scales = [1.0 / math.sqrt(width) for width in WIDTHS]
-    teacher_or = tt[...]
-    chosen = teacher_or >= 0.0
-    teacher = jnp.where(chosen, teacher_or, 0.0)
-    columns = [None] * 13
-    for level in range(4):
-        logits = lv[level] * scales[level]
-        top = jnp.max(jnp.where(chosen, logits, -BIG), axis=1, keepdims=True)
-        shifted = jnp.where(chosen, logits - top, 0.0)
-        weight = jnp.where(chosen, jnp.exp(shifted), 0.0)
-        lv[level] = weight
-        columns[level] = top
-        columns[4 + level] = jnp.sum(weight, axis=1, keepdims=True)
-        columns[8 + level] = jnp.sum(teacher * shifted, axis=1, keepdims=True)
-    columns[12] = jnp.sum(teacher, axis=1, keepdims=True)
-    place_of = lax.broadcasted_iota(jnp.int32, (2 * ROWS, LANES), 1)
-    table = jnp.zeros((2 * ROWS, LANES), F32)
-    for index, value in enumerate(columns):
-        table = jnp.where(place_of == index, value, table)
-    st[...] = table
-    stats_copy = remote(st, sr, sibling)
-    stats_copy.wait_recv()
-    received = sr[...]
-    swapped = jnp.concatenate([received[ROWS:], received[:ROWS]], axis=0)
-    loss_rows = jnp.zeros((ROWS, 1), F32)
-    teacher_sum = (columns[12] + swapped[:, 12:13])[:ROWS]
-    tail = None
-    for level in (3, 2, 1, 0):
-        top, top_other = columns[level], swapped[:, level : level + 1]
+    strip_lane = lax.broadcasted_iota(jnp.int32, (STRIP, LANES), 1)
+
+    def tabulate(columns):
+        table = jnp.zeros((STRIP, LANES), F32)
+        for index, value in enumerate(columns):
+            table = jnp.where(strip_lane == index, value, table)
+        return table
+
+    def gather_terms(first):
+        rows = pl.ds(first, STRIP)
+        teacher_or = tt[rows]
+        chosen = teacher_or >= 0.0
+        teacher = jnp.where(chosen, teacher_or, 0.0)
+        tops, sums, parts = [], [], []
+        for level in range(4):
+            logits = lv[level, rows] * scales[level]
+            top = jnp.max(jnp.where(chosen, logits, -BIG), axis=1, keepdims=True)
+            shifted = jnp.where(chosen, logits - top, 0.0)
+            weight = jnp.where(chosen, jnp.exp(shifted), 0.0)
+            lv[level, rows] = weight
+            tops.append(top)
+            sums.append(jnp.sum(weight, axis=1, keepdims=True))
+            parts.append(jnp.sum(teacher * shifted, axis=1, keepdims=True))
+        parts.append(jnp.sum(teacher, axis=1, keepdims=True))
+        st[0, rows] = tabulate(tops)
+        st[1, rows] = tabulate(sums)
+        st[2, rows] = tabulate(parts)
+
+    stats_copies = []
+    for half in range(2):
+        for first in range(half * ROWS, (half + 1) * ROWS, STRIP):
+            gather_terms(first)
+        here, there = pl.ds(half * ROWS, ROWS), pl.ds((1 - half) * ROWS, ROWS)
+        stats_copies.append(remote(st.at[:, here], sr.at[:, there], sibling))
+
+    loss_strips = []
+
+    def finish_terms(first):
+        rows = pl.ds(first, STRIP)
+        top, top_other = st[0, rows], sr[0, rows]
         peak = jnp.maximum(top, top_other)
         fade, fade_other = jnp.exp(top - peak), jnp.exp(top_other - peak)
-        total = columns[4 + level] * fade + swapped[:, 4 + level : 5 + level] * fade_other
-        part = columns[8 + level] + columns[12] * (top - peak)
-        part_other = swapped[:, 8 + level : 9 + level] + swapped[:, 12:13] * (top_other - peak)
-        loss_rows += jnp.log(total[:ROWS]) * teacher_sum - (part + part_other)[:ROWS]
-        dlogit = (lv[level] * (fade / total) - teacher) * scales[level]
-        tail = dlogit if tail is None else dlogit + tail
-        grid[level] = tail.astype(BF16)
-    diagonal = lax.broadcasted_iota(jnp.int32, (ROWS, LANES), 0) == lax.broadcasted_iota(
-        jnp.int32, (ROWS, LANES), 1
-    )
-    loss_rows += 4.0 * entropy[0]
-    loss[...] = jnp.sum(jnp.where(diagonal, loss_rows, 0.0), axis=0, keepdims=True)
+        total = st[1, rows] * fade + sr[1, rows] * fade_other
+        factor = fade / total
+        if first < ROWS:
+            weight, weight_other = st[2, rows][:, 4:5], sr[2, rows][:, 4:5]
+            part = st[2, rows] + weight * (top - peak) + sr[2, rows] + weight_other * (top_other - peak)
+            terms = jnp.log(total) * (weight + weight_other) - part
+            loss_strips.append(
+                jnp.sum(jnp.where(strip_lane < 4, terms, 0.0), axis=1, keepdims=True)
+            )
+        teacher = jnp.maximum(tt[rows], 0.0)
+        tail = None
+        for level in (3, 2, 1, 0):
+            dlogit = (lv[level, rows] * factor[:, level : level + 1] - teacher) * scales[level]
+            tail = dlogit if tail is None else dlogit + tail
+            grid[level, rows] = tail.astype(BF16)
+
+    for half in (1, 0):
+        stats_copies[1 - half].wait_recv()
+        for first in range(half * ROWS, (half + 1) * ROWS, STRIP):
+            finish_terms(first)
 
 
     pa, pab, pb, pbb, pc, pcb = (buf[k] for k in ("pa", "pab", "pb", "pbb", "pc", "pcb"))
@@ -384,21 +409,60 @@
     rings = {(way, dxl): ring(way, 1, dxl) for dxl in range(2) for way in (1, -1)}
     gb, gbb, rbx, rby = (buf[k] for k in ("gb", "gbb", "rbx", "rby"))
     gc, gcb, rcy, rcx = (buf[k] for k in ("gc", "gcb", "rcy", "rcx"))
-    b_copies, c_copies = [], []
-    for start, count in CHUNKS:
-        part = pl.ds(start, count)
-        b_copies.append(
-            [
-                remote(pbb.at[d % 2, toward(d), :, part], rbx.at[d - 1, :, part], by_x[d])
-                for d in (2, 1, 3)
-            ]
-        )
-        c_copies.append(
-            [
-                remote(pcb.at[(y + d) % NY, :, :, part], rcy.at[d - 1, :, :, part], by_y[d])
-                for d in (2, 1, 3)
-            ]
-        )
+    rbr, rcr = buf["rbr"], buf["rcr"]
+    b_far, c_far, b_copies, c_copies = [], [], [[], []], [[], []]
+
+    def opposite(chunk):
+        part = pl.ds(*CHUNKS[chunk])
+        for copies, ring_of, source, sink in (
+            (b_far, by_x, lambda h: pbb.at[0, toward(2), pl.ds(2 * h, 2), part], rbr),
+            (c_far, by_y, lambda h: pcb.at[(y + 2) % NY, h, :, part], rcr),
+        ):
+            copies.append(
+                [remote(source(h), sink.at[h, :, part], ring_of[1 + 2 * h]) for h in (0, 1)]
+            )
+
+    def direct(chunk):
+        part = pl.ds(*CHUNKS[chunk])
+        for h, d in ((1, 1), (0, 3)):
+            b_copies[chunk].append(
+                remote(
+                    pbb.at[1, toward(d), pl.ds(2 * h, 2), part],
+                    rbx.at[1 - h, pl.ds(2 * h, 2), part],
+                    by_x[d],
+                )
+            )
+            c_copies[chunk].append(
+                remote(pcb.at[(y + d) % NY, h, :, part], rcy.at[1 - h, h, :, part], by_y[d])
+            )
+
+    def relay(chunk):
+        part = pl.ds(*CHUNKS[chunk])
+        arrived(b_far[chunk])
+        for h, d in ((0, 1), (1, 3)):
+            half = pl.ds(2 * h, 2)
+            total = pb[1, toward(d), half, part] + rbr[h, :, part].astype(F32)
+            pbb[1, toward(d), half, part] = total.astype(BF16)
+            b_copies[chunk].append(
+                remote(pbb.at[1, toward(d), half, part], rbx.at[h, half, part], by_x[d])
+            )
+        arrived(c_far[chunk])
+        for h, d in ((0, 1), (1, 3)):
+            to = (y + d) % NY
+            total = pc[to, h, :, part] + rcr[h, :, part].astype(F32)
+            pcb[to, h, :, part] = total.astype(BF16)
+            c_copies[chunk].append(
+                remote(pcb.at[to, h, :, part], rcy.at[h, h, :, part], by_y[d])
+            )
+
+    opposite(0)
+    direct(0)
+
+    diagonal = lax.broadcasted_iota(jnp.int32, (ROWS, LANES), 0) == lax.broadcasted_iota(
+        jnp.int32, (ROWS, LANES), 1
+    )
+    loss_rows = 4.0 * entropy[0] + jnp.concatenate(loss_strips, axis=0)
+    loss[...] = jnp.sum(jnp.where(diagonal, loss_rows, 0.0), axis=0, keepdims=True)
 
     def dot_plain(a, b):
         return jnp.dot(a, b, preferred_element_type=F32)
@@ -419,8 +483,6 @@
         keep_query(cols, dot_plain(grid[3], ws[:, cols]))
         return carry
 
-    lax.fori_loop(2, E // BLOCK, query_step, 0)
-    query_copy = remote(gs, gr, sibling)
 
     def ring_step(step):
         for dxl in range(2):
@@ -450,7 +512,7 @@
     def b_second(chunk):
         part = pl.ds(*CHUNKS[chunk])
         arrived(b_copies[chunk])
-        total = three(pb[0, xh, :, part], rbx[:, :, part])
+        total = pb[0, xh, :, part] + rbx[0, :, part].astype(F32) + rbx[1, :, part].astype(F32)
         gb[:, part] = total
         gbb[:, part] = total.astype(BF16)
         return [
@@ -460,7 +522,8 @@
     def c_second(chunk):
         part = pl.ds(*CHUNKS[chunk])
         arrived(c_copies[chunk])
-        total = three(pc[y, :, :, part], rcy[:, :, :, part])
+        total = pc[y, :, :, part] + rcy[0, :, :, part].astype(F32)
+        total += rcy[1, :, :, part].astype(F32)
         gc[:, :, part] = total
         gcb[:, :, part] = total.astype(BF16)
         return [
@@ -474,7 +537,7 @@
         copies = []
         for at in range(start, start + count):
             dz = (at + FIRST_Z) % NZ
-            if dz and chunk == 0:
+            if dz in FAR:
                 copies.append(remote(narrow.at[at], narrow_in.at[at], by_z[dz]))
             elif dz:
                 copies.append(remote(wide.at[at], wide_in.at[at], by_z[dz]))
@@ -493,20 +556,26 @@
         arrived(c_next[chunk])
         return third(chunk, three(gc[0, xh, part], rcx[:, part]), hc, hcb, rcz, rczb)
 
+    b_next, c_next, last_copies = [None, None], [None, None], []
+    relay(0)
+    opposite(1)
+    direct(1)
     ring_step(1)
     ring_step(2)
+    lax.fori_loop(2, E // BLOCK, query_step, 0)
+    query_copy = remote(gs, gr, sibling)
+    b_next[0] = b_second(0)
+    c_next[0] = c_second(0)
+    ring_step(3)
+    relay(1)
+    last_copies += b_third(0)
+    last_copies += c_third(0)
+    ax_copies = ring_end()
+    b_next[1] = b_second(1)
+    c_next[1] = c_second(1)
     query_copy.wait_recv()
     go[...] += gr[...]
     out_copy = local(go, grad_queries)
-    ring_step(3)
-    b_next, c_next, last_copies = [None, None], [None, None], []
-    b_next[0] = b_second(0)
-    c_next[0] = c_second(0)
-    ax_copies = ring_end()
-    last_copies += b_third(0)
-    last_copies += c_third(0)
-    b_next[1] = b_second(1)
-    c_next[1] = c_second(1)
     arrived(ax_copies)
     ga[...] = three(fa[0, xh], rax)
     ay_copies = [remote(ga.at[(y + d) % NY], ray.at[d - 1], by_y[d]) for d in (1, 2, 3)]
@@ -519,7 +588,7 @@
     at_home = (0 - FIRST_Z) % NZ
     total_b, total_c = hb[at_home], hc[at_home]
     for at in range(NZ):
-        if at < CHUNKS[0][1]:
+        if (at + FIRST_Z) % NZ in FAR:
             total_b += rbzb[at].astype(F32)
             total_c += rczb[at].astype(F32)
         elif at != at_home:
@@ -559,8 +628,41 @@
     )(queries, passages, candidates, scores)
 
 
+def finish_kernel(*refs):
+    sources, sinks, stages, sems = refs[:3], refs[3:6], refs[6:9], refs[9]
+    pieces = [(0, pl.ds(first, PIECE)) for first in range(0, ROWS, PIECE)]
+    pieces += [(1, slice(None)), (2, slice(None))]
+    loads, stores = [], []
+    for index, (which, rows) in enumerate(pieces):
+        source, stage, sink = sources[which], stages[which], sinks[which]
+        loads.append(pltpu.make_async_copy(source.at[rows], stage.at[rows], sems.at[0, index]))
+        stores.append(pltpu.make_async_copy(stage.at[rows], sink.at[rows], sems.at[1, index]))
+    for copy in loads:
+        copy.start()
+    for load, store in zip(loads, stores):
+        load.wait()
+        store.start()
+    for copy in stores:
+        copy.wait()
+
+
+def finish(*arrays):
+    anywhere = pl.BlockSpec(memory_space=pl.ANY)
+    return pl.pallas_call(
+        finish_kernel,
+        out_shape=tuple(jax.ShapeDtypeStruct(a.shape, a.dtype) for a in arrays),
+        in_specs=[anywhere] * 3,
+        out_specs=(anywhere,) * 3,
+        scratch_shapes=[pltpu.VMEM(a.shape, a.dtype) for a in arrays]
+        + [pltpu.SemaphoreType.DMA((2, ROWS // PIECE + 2))],
+        compiler_params=pltpu.CompilerParams(vmem_limit_bytes=60 * 2**20),
+        name="finish",
+    )(*arrays)
+
+
 def shards(queries, passages, candidates, teacher_scores):
     loss, grad_queries, grad_passages = main_call(queries, passages, candidates, teacher_scores)
+    grad_queries, grad_passages, loss = finish(grad_queries, grad_passages, loss)
     return (loss.reshape(ROWS), grad_queries, grad_passages)
 
 

time: 80.8 us -> 75.3 us (0.932)
  local copies, waits for them, and re-layouts: 4.89 us -> 0 us
  Pallas kernels: 75.2 us -> 74.2 us
    unnamed x5 -> x0, local copies, waits for them, and re-layouts: 4.89 us -> none
    pallas_call x1, Pallas kernels: 75.2 us -> 71.8 us  [main_call(): pl.pallas_call(main_kernel, out_shape=(jax.ShapeDtypeStruct((1, ROWS), F3...]
    pallas_call x0 -> x1, Pallas kernels: none -> 2.45 us  [finish(): pl.pallas_call(finish_kernel, out_shape=tuple((jax.ShapeDtypeStruct(a.sha...]
where the time goes in v3:
time: 75.3 us; the launch traced here: 74.9 us
  Pallas kernels  74.2 us (99%)
    pallas_call x1, Pallas kernels, main_call(): pl.pallas_call(main_kernel, out_shape=(jax.ShapeDtypeStruct((1, ROWS), F3...  71.8 us
    pallas_call x1, Pallas kernels, finish(): pl.pallas_call(finish_kernel, out_shape=tuple((jax.ShapeDtypeStruct(a.sha...  2.45 us

profile of v3, /device:TPU:1, one launch (start us, length us, event | category | flops | bytes accessed | tf_op | source)
XLA Modules:
  0.0 74.9 jit_solution(11829814910511236317)
XLA Ops:
  0.6 71.8 %distill.1 = (f32[1,128]{1,0:T(1,128)}, f32[128,4096]{1,0:T(8,128)}, f32[32,512]{1,0:T(8,128)}) custom-call(bf16[128,4096]{1,0:T(8,128)(2,1)} %queries.1, bf16[32,4096]{1,0:T(8,128)(2,1)} %passages.1, s32[128,128]{1,0:T(8,128)} %candidates.1, f32[128,128]{1,0:T(8,128)} %scores.1), custom_call_target="tpu_custom_call" | custom-call | tf_op jit(solution)/shard_map/distill/pallas_call | solution.py:614
  72.4 2.4 %finish.1 = (f32[128,4096]{1,0:T(8,128)}, f32[32,512]{1,0:T(8,128)}, f32[1,128]{1,0:T(1,128)}) custom-call(f32[128,4096]{1,0:T(8,128)} %get-tuple-element.9.refs_0_, f32[32,512]{1,0:T(8,128)} %get-tuple-element.10.refs_1_, f32[1,128]{1,0:T(1,128)} %get-tuple-element.11.refs_2_), custom_call_target="tpu_custom_call" | custom-call | tf_op jit(solution)/shard_map/finish/pallas_call | solution.py:651

commit v4 on v3

--- a/solution.py
+++ b/solution.py
@@ -24,7 +24,7 @@
 LANES = 128
 BIG = 3.0e38
 PIECE = 16
-STRIP = 32
+STRIP = 128
 
 QUARTER = 384
 FLAT = E - 4 * QUARTER
@@ -59,11 +59,12 @@
     cs=((2 * ROWS, LANES), jnp.int32),
     rs=((2 * ROWS, LANES), F32),
     ts=((2 * ROWS, LANES), F32),
-    tt=((2 * ROWS, POOL), F32),
-    lv=((4, 2 * ROWS, POOL), F32),
-    st=((3, 2 * ROWS, LANES), F32),
-    sr=((3, 2 * ROWS, LANES), F32),
-    grid=((4, 2 * ROWS, POOL), BF16),
+    tt=((POOL, 2 * ROWS), F32),
+    lv=((4, POOL, 2 * ROWS), F32),
+    st=((2, 3, 8, ROWS), F32),
+    sr=((2, 3, 8, ROWS), F32),
+    grid=((4, POOL, 2 * ROWS), BF16),
+    turned=((4, 2 * ROWS, POOL), BF16),
     go=((ROWS, E), F32),
     gs=((ROWS, E), F32),
     gr=((ROWS, E), F32),
@@ -233,7 +234,7 @@
             position = jnp.where(probe < target, position + step, position)
         hit = jnp.take_along_axis(chosen, position, axis=1) == target
         value = jnp.take_along_axis(ts[rows], position, axis=1)
-        tt[rows, chunk * LANES : (chunk + 1) * LANES] = jnp.where(hit, value, -1.0)
+        tt[chunk * LANES : (chunk + 1) * LANES, rows] = jnp.where(hit, value, -1.0).T
 
     own, other = pl.ds(0, ROWS), pl.ds(ROWS, ROWS)
     chores = [lambda: (arrived_here(own_teacher), teach(own))]
@@ -273,95 +274,99 @@
                 if key not in x_done:
                     from_x(*key)
         arrived(y_copies[dxl])
-        if dxl == 1:
-            pass
         rows = pl.ds(dxl * GROUP, GROUP)
         head = qs[:, 0:W2]
         zero = jnp.zeros_like(head)
         narrow = ws[rows, 0:W2]
-        level = dot_rows(jnp.where(column < W1, head, zero), narrow)
-        lv[0, :, rows] = level
-        level += dot_rows(jnp.where(column < W1, zero, head), narrow)
-        lv[1, :, rows] = level
-        level += dot_rows(qs[:, W2:W3], ws[rows, W2:W3])
-        lv[2, :, rows] = level
+        level = dot_rows(narrow, jnp.where(column < W1, head, zero))
+        lv[0, rows] = level
+        level += dot_rows(narrow, jnp.where(column < W1, zero, head))
+        lv[1, rows] = level
+        level += dot_rows(ws[rows, W2:W3], qs[:, W2:W3])
+        lv[2, rows] = level
 
         def score_step(index, total, rows=rows):
             cols = pl.ds(pl.multiple_of(index * 1024, 1024), 1024)
-            return total + dot_rows(qs[:, cols], ws[rows, cols])
-
-        lv[3, :, rows] = lax.fori_loop(1, E // 1024, score_step, level)
+            return total + dot_rows(ws[rows, cols], qs[:, cols])
+
+        lv[3, rows] = lax.fori_loop(1, E // 1024, score_step, level)
 
 
     scales = [1.0 / math.sqrt(width) for width in WIDTHS]
-    strip_lane = lax.broadcasted_iota(jnp.int32, (STRIP, LANES), 1)
-
-    def tabulate(columns):
-        table = jnp.zeros((STRIP, LANES), F32)
-        for index, value in enumerate(columns):
-            table = jnp.where(strip_lane == index, value, table)
-        return table
-
-    def gather_terms(first):
-        rows = pl.ds(first, STRIP)
-        teacher_or = tt[rows]
-        chosen = teacher_or >= 0.0
-        teacher = jnp.where(chosen, teacher_or, 0.0)
+    strips = [pl.ds(first, STRIP) for first in range(0, POOL, STRIP)]
+
+    def tabulate(rows):
+        rows = rows + [jnp.zeros((1, ROWS), F32)] * (8 - len(rows))
+        return jnp.concatenate(rows, axis=0)
+
+    def gather_terms(half):
+        lanes = pl.ds(half * ROWS, ROWS)
         tops, sums, parts = [], [], []
+        weight_sum = jnp.zeros((1, ROWS), F32)
+        for strip in strips:
+            weight_sum += jnp.sum(jnp.maximum(tt[strip, lanes], 0.0), axis=0, keepdims=True)
         for level in range(4):
-            logits = lv[level, rows] * scales[level]
-            top = jnp.max(jnp.where(chosen, logits, -BIG), axis=1, keepdims=True)
-            shifted = jnp.where(chosen, logits - top, 0.0)
-            weight = jnp.where(chosen, jnp.exp(shifted), 0.0)
-            lv[level, rows] = weight
+            top = jnp.full((1, ROWS), -BIG, F32)
+            for strip in strips:
+                logits = jnp.where(
+                    tt[strip, lanes] >= 0.0, lv[level, strip, lanes] * scales[level], -BIG
+                )
+                lv[level, strip, lanes] = logits
+                top = jnp.maximum(top, jnp.max(logits, axis=0, keepdims=True))
+            total = jnp.zeros((1, ROWS), F32)
+            part = jnp.zeros((1, ROWS), F32)
+            for strip in strips:
+                shifted = lv[level, strip, lanes] - top
+                weight = jnp.exp(shifted)
+                lv[level, strip, lanes] = weight
+                total += jnp.sum(weight, axis=0, keepdims=True)
+                teacher = jnp.maximum(tt[strip, lanes], 0.0)
+                part += jnp.sum(teacher * shifted, axis=0, keepdims=True)
             tops.append(top)
-            sums.append(jnp.sum(weight, axis=1, keepdims=True))
-            parts.append(jnp.sum(teacher * shifted, axis=1, keepdims=True))
-        parts.append(jnp.sum(teacher, axis=1, keepdims=True))
-        st[0, rows] = tabulate(tops)
-        st[1, rows] = tabulate(sums)
-        st[2, rows] = tabulate(parts)
+            sums.append(total)
+            parts.append(part)
+        st[half, 0] = tabulate(tops)
+        st[half, 1] = tabulate(sums)
+        st[half, 2] = tabulate(parts + [weight_sum])
 
     stats_copies = []
     for half in range(2):
-        for first in range(half * ROWS, (half + 1) * ROWS, STRIP):
-            gather_terms(first)
-        here, there = pl.ds(half * ROWS, ROWS), pl.ds((1 - half) * ROWS, ROWS)
-        stats_copies.append(remote(st.at[:, here], sr.at[:, there], sibling))
-
-    loss_strips = []
-
-    def finish_terms(first):
-        rows = pl.ds(first, STRIP)
-        top, top_other = st[0, rows], sr[0, rows]
+        gather_terms(half)
+        stats_copies.append(remote(st.at[half], sr.at[1 - half], sibling))
+
+    loss_terms = []
+
+    def finish_terms(half):
+        lanes = pl.ds(half * ROWS, ROWS)
+        top, top_other = st[half, 0], sr[half, 0]
         peak = jnp.maximum(top, top_other)
         fade, fade_other = jnp.exp(top - peak), jnp.exp(top_other - peak)
-        total = st[1, rows] * fade + sr[1, rows] * fade_other
+        total = st[half, 1] * fade + sr[half, 1] * fade_other
         factor = fade / total
-        if first < ROWS:
-            weight, weight_other = st[2, rows][:, 4:5], sr[2, rows][:, 4:5]
-            part = st[2, rows] + weight * (top - peak) + sr[2, rows] + weight_other * (top_other - peak)
+        if half == 0:
+            part, part_other = st[half, 2], sr[half, 2]
+            weight, weight_other = part[4:5], part_other[4:5]
+            part = part + weight * (top - peak) + part_other + weight_other * (top_other - peak)
             terms = jnp.log(total) * (weight + weight_other) - part
-            loss_strips.append(
-                jnp.sum(jnp.where(strip_lane < 4, terms, 0.0), axis=1, keepdims=True)
-            )
-        teacher = jnp.maximum(tt[rows], 0.0)
-        tail = None
-        for level in (3, 2, 1, 0):
-            dlogit = (lv[level, rows] * factor[:, level : level + 1] - teacher) * scales[level]
-            tail = dlogit if tail is None else dlogit + tail
-            grid[level, rows] = tail.astype(BF16)
+            loss_terms.append(jnp.sum(terms[:4], axis=0, keepdims=True))
+        for strip in strips:
+            teacher = jnp.maximum(tt[strip, lanes], 0.0)
+            tail = None
+            for level in (3, 2, 1, 0):
+                student = lv[level, strip, lanes] * factor[level : level + 1]
+                dlogit = (student - teacher) * scales[level]
+                tail = dlogit if tail is None else dlogit + tail
+                grid[level, strip, lanes] = tail.astype(BF16)
 
     for half in (1, 0):
         stats_copies[1 - half].wait_recv()
-        for first in range(half * ROWS, (half + 1) * ROWS, STRIP):
-            finish_terms(first)
+        finish_terms(half)
 
 
     pa, pab, pb, pbb, pc, pcb = (buf[k] for k in ("pa", "pab", "pb", "pbb", "pc", "pcb"))
 
-    def dot_columns(a, b):
-        return lax.dot_general(a, b, (((0,), (0,)), ((), ())), preferred_element_type=F32)
+    def dot_plain(a, b):
+        return jnp.dot(a, b, preferred_element_type=F32)
 
     def keep(dxl, q, result):
         rounded = result.astype(BF16)
@@ -378,20 +383,6 @@
             pc[y_of, dxl, xh_of, at] = result[low, WA:]
             pcb[y_of, dxl, xh_of, at] = rounded[low, WA:]
 
-    for dxl in range(2):
-        part = pl.ds(dxl * GROUP, GROUP)
-        narrow = lax.broadcasted_iota(jnp.int32, (GROUP, W2), 1) < W1
-        first = qs[:, 0:W2]
-        first = jnp.where(
-            narrow, dot_columns(grid[0, :, part], first), dot_columns(grid[1, :, part], first)
-        )
-        second = dot_columns(grid[2, :, part], qs[:, W2:BLOCK])
-        keep(dxl, 0, jnp.concatenate([first, second], axis=1))
-        keep(dxl, 1, dot_columns(grid[2, :, part], qs[:, BLOCK : 2 * BLOCK]))
-        for q in range(2, 8):
-            keep(dxl, q, dot_columns(grid[3, :, part], qs[:, q * BLOCK : (q + 1) * BLOCK]))
-
-
     ra, rax, ray, fa, ga = (buf[k] for k in ("ra", "rax", "ray", "fa", "ga"))
 
     def ring(way, step, dxl):
@@ -406,21 +397,29 @@
     def toward(d):
         return ((x + d) % NX) // 2
 
-    rings = {(way, dxl): ring(way, 1, dxl) for dxl in range(2) for way in (1, -1)}
+    rings = {}
     gb, gbb, rbx, rby = (buf[k] for k in ("gb", "gbb", "rbx", "rby"))
     gc, gcb, rcy, rcx = (buf[k] for k in ("gc", "gcb", "rcy", "rcx"))
     rbr, rcr = buf["rbr"], buf["rcr"]
     b_far, c_far, b_copies, c_copies = [], [], [[], []], [[], []]
 
-    def opposite(chunk):
-        part = pl.ds(*CHUNKS[chunk])
-        for copies, ring_of, source, sink in (
-            (b_far, by_x, lambda h: pbb.at[0, toward(2), pl.ds(2 * h, 2), part], rbr),
-            (c_far, by_y, lambda h: pcb.at[(y + 2) % NY, h, :, part], rcr),
-        ):
-            copies.append(
-                [remote(source(h), sink.at[h, :, part], ring_of[1 + 2 * h]) for h in (0, 1)]
-            )
+    def opposite_b(chunk):
+        part = pl.ds(*CHUNKS[chunk])
+        b_far.append(
+            [
+                remote(pbb.at[0, toward(2), pl.ds(2 * h, 2), part], rbr.at[h, :, part], by_x[d])
+                for h, d in ((0, 1), (1, 3))
+            ]
+        )
+
+    def opposite_c(chunk):
+        part = pl.ds(*CHUNKS[chunk])
+        c_far.append(
+            [
+                remote(pcb.at[(y + 2) % NY, h, :, part], rcr.at[h, :, part], by_y[d])
+                for h, d in ((0, 1), (1, 3))
+            ]
+        )
 
     def direct(chunk):
         part = pl.ds(*CHUNKS[chunk])
@@ -455,17 +454,34 @@
                 remote(pcb.at[to, h, :, part], rcy.at[h, h, :, part], by_y[d])
             )
 
-    opposite(0)
+    for dxl in range(2):
+        part = pl.ds(dxl * GROUP, GROUP)
+        narrow = lax.broadcasted_iota(jnp.int32, (GROUP, W2), 1) < W1
+        first = qs[:, 0:W2]
+        first = jnp.where(
+            narrow, dot_plain(grid[0, part], first), dot_plain(grid[1, part], first)
+        )
+        second = dot_plain(grid[2, part], qs[:, W2:BLOCK])
+        keep(dxl, 0, jnp.concatenate([first, second], axis=1))
+        keep(dxl, 1, dot_plain(grid[2, part], qs[:, BLOCK : 2 * BLOCK]))
+        for q in range(2, 8):
+            keep(dxl, q, dot_plain(grid[3, part], qs[:, q * BLOCK : (q + 1) * BLOCK]))
+        for way in (1, -1):
+            rings[way, dxl] = ring(way, 1, dxl)
+        if dxl == 0:
+            opposite_b(0)
+    opposite_c(0)
     direct(0)
 
     diagonal = lax.broadcasted_iota(jnp.int32, (ROWS, LANES), 0) == lax.broadcasted_iota(
         jnp.int32, (ROWS, LANES), 1
     )
-    loss_rows = 4.0 * entropy[0] + jnp.concatenate(loss_strips, axis=0)
-    loss[...] = jnp.sum(jnp.where(diagonal, loss_rows, 0.0), axis=0, keepdims=True)
-
-    def dot_plain(a, b):
-        return jnp.dot(a, b, preferred_element_type=F32)
+    entropy_row = jnp.sum(jnp.where(diagonal, entropy[0], 0.0), axis=0, keepdims=True)
+    loss[...] = 4.0 * entropy_row + loss_terms[0]
+
+    turned = buf["turned"]
+    for level in range(4):
+        turned[level] = grid[level].T
 
     def keep_query(cols, result):
         go[:, cols] = result[:ROWS]
@@ -473,14 +489,14 @@
 
     first = ws[:, 0:W2]
     keep_query(
-        slice(0, W2), jnp.where(column < W1, dot_plain(grid[0], first), dot_plain(grid[1], first))
+        slice(0, W2), jnp.where(column < W1, dot_plain(turned[0], first), dot_plain(turned[1], first))
     )
-    keep_query(slice(W2, BLOCK), dot_plain(grid[2], ws[:, W2:BLOCK]))
-    keep_query(slice(BLOCK, W3), dot_plain(grid[2], ws[:, BLOCK:W3]))
+    keep_query(slice(W2, BLOCK), dot_plain(turned[2], ws[:, W2:BLOCK]))
+    keep_query(slice(BLOCK, W3), dot_plain(turned[2], ws[:, BLOCK:W3]))
 
     def query_step(index, carry):
         cols = pl.ds(pl.multiple_of(index * BLOCK, BLOCK), BLOCK)
-        keep_query(cols, dot_plain(grid[3], ws[:, cols]))
+        keep_query(cols, dot_plain(turned[3], ws[:, cols]))
         return carry
 
 
@@ -558,7 +574,8 @@
 
     b_next, c_next, last_copies = [None, None], [None, None], []
     relay(0)
-    opposite(1)
+    opposite_b(1)
+    opposite_c(1)
     direct(1)
     ring_step(1)
     ring_step(2)

time: 75.3 us -> 74.1 us (0.984)
  Pallas kernels: 74.2 us -> 72.6 us
    pallas_call x1, Pallas kernels: 71.8 us -> 70.1 us  [main_call(): pl.pallas_call(main_kernel, out_shape=(jax.ShapeDtypeStruct((1, ROWS), F3...]
where the time goes in v4:
time: 74.1 us; the launch traced here: 73.2 us
  Pallas kernels  72.6 us (98%)
    pallas_call x1, Pallas kernels, main_call(): pl.pallas_call(main_kernel, out_shape=(jax.ShapeDtypeStruct((1, ROWS), F3...  70.1 us
    pallas_call x1, Pallas kernels, finish(): pl.pallas_call(finish_kernel, out_shape=tuple((jax.ShapeDtypeStruct(a.sha...  2.45 us

profile of v4, /device:TPU:1, one launch (start us, length us, event | category | flops | bytes accessed | tf_op | source)
XLA Modules:
  0.0 73.2 jit_solution(143540894693740163)
XLA Ops:
  0.6 70.1 %distill.1 = (f32[1,128]{1,0:T(1,128)}, f32[128,4096]{1,0:T(8,128)}, f32[32,512]{1,0:T(8,128)}) custom-call(bf16[128,4096]{1,0:T(8,128)(2,1)} %queries.1, bf16[32,4096]{1,0:T(8,128)(2,1)} %passages.1, s32[128,128]{1,0:T(8,128)} %candidates.1, f32[128,128]{1,0:T(8,128)} %scores.1), custom_call_target="tpu_custom_call" | custom-call | tf_op jit(solution)/shard_map/distill/pallas_call | solution.py:631
  70.8 2.4 %finish.1 = (f32[128,4096]{1,0:T(8,128)}, f32[32,512]{1,0:T(8,128)}, f32[1,128]{1,0:T(1,128)}) custom-call(f32[128,4096]{1,0:T(8,128)} %get-tuple-element.9.refs_0_, f32[32,512]{1,0:T(8,128)} %get-tuple-element.10.refs_1_, f32[1,128]{1,0:T(1,128)} %get-tuple-element.11.refs_2_), custom_call_target="tpu_custom_call" | custom-call | tf_op jit(solution)/shard_map/finish/pallas_call | solution.py:668

commit v5 on v4

--- a/solution.py
+++ b/solution.py
@@ -72,9 +72,12 @@
     pab=((NZ, 2, 8, SPAN, WA), BF16),
     ra=((2, 4, 2, 8, SPAN, WA), BF16),
     fa=((2, 2, 4, SPAN, WA), F32),
-    rax=((3, 4, SPAN, WA), F32),
-    ga=((4, SPAN, WA), F32),
-    ray=((3, SPAN, WA), F32),
+    rax=((3, 4, HALF, WA), F32),
+    ga=((4, HALF, WA), F32),
+    ray=((3, HALF, WA), F32),
+    ray_low=((3, 2, 2, HALF, WA), F32),
+    ga_low=((2, 2, HALF, WA), F32),
+    rax_low=((3, HALF, WA), F32),
     pb=((2, 2, 4, NZ, HALF, WB), F32),
     pbb=((2, 2, 4, NZ, HALF, WB), BF16),
     rbr=((2, 2, NZ, HALF, WB), BF16),
@@ -181,7 +184,7 @@
 
     def along_y(dxl, dz):
         here = ws.at[pl.ds(row(dxl, dz), SPAN), mine]
-        for d in (1, 3, 2):
+        for d in (2, 1, 3):
             y_copies[dxl].append(remote(here, here, by_y[d]))
 
     def arrived_here(copies):
@@ -250,8 +253,8 @@
         for way in (1, -1):
             z_copies[piece, step, way].wait_recv()
             if step < 4:
+                along_x(piece, -way * step)
                 along_z(piece, step, way)
-                along_x(piece, -way * step)
                 if piece == "m":
                     along_y(0, -way * step)
         if step == 4:
@@ -384,6 +387,7 @@
             pcb[y_of, dxl, xh_of, at] = rounded[low, WA:]
 
     ra, rax, ray, fa, ga = (buf[k] for k in ("ra", "rax", "ray", "fa", "ga"))
+    ray_low, ga_low, rax_low = (buf[k] for k in ("ray_low", "ga_low", "rax_low"))
 
     def ring(way, step, dxl):
         dz = (way * (5 - step)) % NZ
@@ -520,7 +524,14 @@
             rings[-1, dxl].wait_recv()
             total = pa[0, dxl] + ra[0, 3, dxl].astype(F32) + ra[1, 3, dxl].astype(F32)
             fa[dxl] = total.reshape(2, 4, SPAN, WA)
-        return [remote(fa.at[d % 2, toward(d)], rax.at[d - 1], by_x[d]) for d in (1, 2, 3)]
+        top, low = pl.ds(0, HALF), pl.ds(HALF, HALF)
+        return (
+            [remote(fa.at[d % 2, toward(d), :, top], rax.at[d - 1], by_x[d]) for d in (2, 1, 3)],
+            [
+                remote(fa.at[:, :, (y + d) % NY, low], ray_low.at[d - 1], by_y[d])
+                for d in (2, 1, 3)
+            ],
+        )
 
     def three(own, parts):
         return own + parts[0].astype(F32) + parts[1].astype(F32) + parts[2].astype(F32)
@@ -587,20 +598,26 @@
     relay(1)
     last_copies += b_third(0)
     last_copies += c_third(0)
-    ax_copies = ring_end()
+    a_copies = ring_end()
     b_next[1] = b_second(1)
     c_next[1] = c_second(1)
+    arrived(a_copies[0])
+    ga[...] = three(fa[0, xh, :, :HALF], rax)
+    a_last = [remote(ga.at[(y + d) % NY], ray.at[d - 1], by_y[d]) for d in (2, 1, 3)]
+    arrived(a_copies[1])
+    ga_low[...] = three(fa[:, :, y, HALF:], ray_low)
+    a_last += [
+        remote(ga_low.at[d % 2, toward(d)], rax_low.at[d - 1], by_x[d]) for d in (2, 1, 3)
+    ]
+    last_copies += b_third(1)
+    last_copies += c_third(1)
     query_copy.wait_recv()
     go[...] += gr[...]
     out_copy = local(go, grad_queries)
-    arrived(ax_copies)
-    ga[...] = three(fa[0, xh], rax)
-    ay_copies = [remote(ga.at[(y + d) % NY], ray.at[d - 1], by_y[d]) for d in (1, 2, 3)]
-    last_copies += b_third(1)
-    last_copies += c_third(1)
-    arrived(ay_copies)
+    arrived(a_last)
     ob = buf["ob"]
-    ob[:, :WA] = three(ga[y], ray)
+    ob[:HALF, :WA] = three(ga[y], ray)
+    ob[HALF:, :WA] = three(ga_low[0, xh], rax_low)
     arrived(last_copies)
     at_home = (0 - FIRST_Z) % NZ
     total_b, total_c = hb[at_home], hc[at_home]

time: 74.1 us -> 72.9 us (0.984)
  no operation moved by 1% of the time
where the time goes in v5:
time: 72.9 us; the launch traced here: 72.7 us
  Pallas kernels  72 us (99%)
    pallas_call x1, Pallas kernels, main_call(): pl.pallas_call(main_kernel, out_shape=(jax.ShapeDtypeStruct((1, ROWS), F3...  69.6 us
    pallas_call x1, Pallas kernels, finish(): pl.pallas_call(finish_kernel, out_shape=tuple((jax.ShapeDtypeStruct(a.sha...  2.45 us

profile of v5, /device:TPU:1, one launch (start us, length us, event | category | flops | bytes accessed | tf_op | source)
XLA Modules:
  0.0 72.7 jit_solution(15437280930312759589)
XLA Ops:
  0.6 69.6 %distill.1 = (f32[1,128]{1,0:T(1,128)}, f32[128,4096]{1,0:T(8,128)}, f32[32,512]{1,0:T(8,128)}) custom-call(bf16[128,4096]{1,0:T(8,128)(2,1)} %queries.1, bf16[32,4096]{1,0:T(8,128)(2,1)} %passages.1, s32[128,128]{1,0:T(8,128)} %candidates.1, f32[128,128]{1,0:T(8,128)} %scores.1), custom_call_target="tpu_custom_call" | custom-call | tf_op jit(solution)/shard_map/distill/pallas_call | solution.py:648
  70.2 2.4 %finish.1 = (f32[128,4096]{1,0:T(8,128)}, f32[32,512]{1,0:T(8,128)}, f32[1,128]{1,0:T(1,128)}) custom-call(f32[128,4096]{1,0:T(8,128)} %get-tuple-element.9.refs_0_, f32[32,512]{1,0:T(8,128)} %get-tuple-element.10.refs_1_, f32[1,128]{1,0:T(1,128)} %get-tuple-element.11.refs_2_), custom_call_target="tpu_custom_call" | custom-call | tf_op jit(solution)/shard_map/finish/pallas_call | solution.py:685

commit v6 on v5

--- a/solution.py
+++ b/solution.py
@@ -276,7 +276,6 @@
             for key in x_copies:
                 if key not in x_done:
                     from_x(*key)
-        arrived(y_copies[dxl])
         rows = pl.ds(dxl * GROUP, GROUP)
         head = qs[:, 0:W2]
         zero = jnp.zeros_like(head)
@@ -289,10 +288,14 @@
         lv[2, rows] = level
 
         def score_step(index, total, rows=rows):
-            cols = pl.ds(pl.multiple_of(index * 1024, 1024), 1024)
+            cols = pl.ds(index * 1024, 1024)
+            if not isinstance(index, int):
+                cols = pl.ds(pl.multiple_of(index * 1024, 1024), 1024)
             return total + dot_rows(ws[rows, cols], qs[:, cols])
 
-        lv[3, rows] = lax.fori_loop(1, E // 1024, score_step, level)
+        level = score_step(1, level)
+        arrived(y_copies[dxl])
+        lv[3, rows] = lax.fori_loop(2, E // 1024, score_step, level)
 
 
     scales = [1.0 / math.sqrt(width) for width in WIDTHS]

time: 72.9 us -> 72.4 us (level)
  no operation moved by 1% of the time
where the time goes in v6:
time: 72.4 us; the launch traced here: 72.1 us
  Pallas kernels  71.3 us (98%)
  between operations  0.8 us (1%)
    pallas_call x1, Pallas kernels, main_call(): pl.pallas_call(main_kernel, out_shape=(jax.ShapeDtypeStruct((1, ROWS), F3...  68.9 us
    pallas_call x1, Pallas kernels, finish(): pl.pallas_call(finish_kernel, out_shape=tuple((jax.ShapeDtypeStruct(a.sha...  2.45 us

profile of v6, /device:TPU:1, one launch (start us, length us, event | category | flops | bytes accessed | tf_op | source)
XLA Modules:
  0.0 72.1 jit_solution(14843954206158050082)
XLA Ops:
  0.6 68.9 %distill.1 = (f32[1,128]{1,0:T(1,128)}, f32[128,4096]{1,0:T(8,128)}, f32[32,512]{1,0:T(8,128)}) custom-call(bf16[128,4096]{1,0:T(8,128)(2,1)} %queries.1, bf16[32,4096]{1,0:T(8,128)(2,1)} %passages.1, s32[128,128]{1,0:T(8,128)} %candidates.1, f32[128,128]{1,0:T(8,128)} %scores.1), custom_call_target="tpu_custom_call" | custom-call | tf_op jit(solution)/shard_map/distill/pallas_call | solution.py:651
  69.5 2.4 %finish.1 = (f32[128,4096]{1,0:T(8,128)}, f32[32,512]{1,0:T(8,128)}, f32[1,128]{1,0:T(1,128)}) custom-call(f32[128,4096]{1,0:T(8,128)} %get-tuple-element.9.refs_0_, f32[32,512]{1,0:T(8,128)} %get-tuple-element.10.refs_1_, f32[1,128]{1,0:T(1,128)} %get-tuple-element.11.refs_2_), custom_call_target="tpu_custom_call" | custom-call | tf_op jit(solution)/shard_map/finish/pallas_call | solution.py:688
